TPU v7x, 128 devices: a whole 4x4x4 slice. The times are simulated.
128 devices in a mesh: dp: 16 (over z, x_lo, core), ctx: 8 (over y, x_hi).
Axes of the slice: x: 4 (x_hi: 2, x_lo: 2; x = x_hi * 2 + x_lo), y: 4, z: 4, core: 2. Of those that a mesh axis runs over, the one named last changes fastest.
Arguments:
- loader_rows: bfloat16 [32768, 512], P(('dp', 'ctx')), may hold values from -60 to 60
- send_slot: int32 [32768], P(('dp', 'ctx')), may hold values from 0 to 383, as said below
- arrive_slot: int32 [32768], P(('dp', 'ctx')), may hold values from 0 to 383, as said below
- user_lengths: int32 [16, 4], P('dp'), may hold values from 1 to 1280, 2048 in all within a row
- proj_weight: bfloat16 [512, 2048], replicated, may hold values from -0.25 to 0.25
- out_weight: bfloat16 [512, 512], replicated, may hold values from -0.25 to 0.25
- cotangent: bfloat16 [32768, 512], P(('dp', 'ctx')), may hold values from -6 to 6
Outputs:
- layer_out: bfloat16 [32768, 512], P(('dp', 'ctx'))
- row_grads: bfloat16 [32768, 512], P(('dp', 'ctx'))
- proj_grad: float32 [512, 2048], replicated
- out_grad: float32 [512, 512], replicated
Inputs may be any that keep to these rules, and one draw needn't show every extreme that they name: `send_slot`: on each loader device its 256 entries are distinct slots d * 3 + k, d the owner device and k counting that owner's rows from this loader from 0; no loader sends more than 3 rows to one owner and some pairs send exactly 3; the number of rows from loader s to owner d depends only on (d - s) mod (16 * 8). `arrive_slot`: on each owner device its 256 entries are distinct slots s * 3 + k, the k-th row that loader s sends to it; every owner receives exactly 256 rows.
All inputs are finite; a program needn't handle non-finite values.
Results may differ from a plain program's by a relative error of at most 0.009.
Values may be sent and summed in bfloat16 or wider, within the bound.
A program may use at most 128 MiB of HBM per device.

v0:
```python
import jax
import jax.numpy as jnp
from jax import lax
from jax.sharding import PartitionSpec as P

HEADS = 8


norm_eps = 1e-05


def normalize(values):
    centre = values - jnp.mean(values, axis=-1, keepdims=True)
    inverse = lax.rsqrt(jnp.mean(centre * centre, axis=-1, keepdims=True) + norm_eps)
    return (centre * inverse, inverse)


def normalize_back(grad_in, normed, inverse):
    mean_grad = jnp.mean(grad_in, axis=-1, keepdims=True)
    mean_cross = jnp.mean(grad_in * normed, axis=-1, keepdims=True)
    return (grad_in - mean_grad - normed * mean_cross) * inverse


def silu_grad(values):
    sigma = jax.nn.sigmoid(values)
    return sigma * (1.0 + values * (1.0 - sigma))


def in_blocks(step_fn, block_rows, running, pieces):
    total_rows = pieces[0].shape[0]

    def one_block(index, carry):
        start = index * block_rows
        sliced = tuple((lax.dynamic_slice_in_dim(each, start, block_rows, 0) for each in pieces))
        return step_fn(carry, sliced, start)

    return lax.fori_loop(0, total_rows // block_rows, one_block, running)


def local(loader_rows, send_slot, arrive_slot, user_lengths, proj_weight, out_weight, cotangent):
    row_count = send_slot.shape[0]
    model_width = out_weight.shape[0]
    head_dim = model_width // HEADS
    score_scale = head_dim ** (-0.5)
    group_size = lax.axis_size("ctx")
    group_count = lax.axis_size("dp")
    device_count = group_size * group_count
    per_pair = row_count // device_count
    capacity = per_pair + max(1, per_pair // 2)
    half_rows = row_count // 2
    group_total = group_size * row_count
    outgoing = (
        jnp.zeros((device_count * capacity, model_width), jnp.bfloat16)
        .at[send_slot]
        .set(loader_rows)
    )
    arrived = lax.all_to_all(
        outgoing.reshape(device_count, capacity, model_width),
        ("dp", "ctx"),
        split_axis=0,
        concat_axis=0,
        tiled=True,
    )
    own_rows = arrived.reshape(device_count * capacity, model_width)[arrive_slot]
    ends = jnp.cumsum(user_lengths[0])

    def position_of(row_index):
        device_of = row_index // row_count
        local_of = row_index % row_count
        return jnp.where(
            local_of < half_rows,
            device_of * half_rows + local_of,
            group_total - (device_of + 1) * half_rows + (local_of - half_rows),
        )

    own_pos = position_of(
        lax.axis_index("ctx") * row_count + jnp.arange(row_count, dtype=jnp.int32)
    )

    def user_of(positions):
        return jnp.sum((ends[None, :] <= positions[:, None]).astype(jnp.int32), axis=1)

    own_users = user_of(own_pos)

    def allowed_of(query_pos, query_users, key_pos, key_users):
        return (key_pos[None, :] <= query_pos[:, None]) & (
            query_users[:, None] == key_users[None, :]
        )

    def split_heads(values):
        return values.reshape(values.shape[0], HEADS, head_dim)

    def merge_heads(values):
        return values.reshape(values.shape[0], model_width)

    def piece_scores(query_part, key_part):
        return (
            jnp.einsum(
                "qhd,khd->hqk",
                split_heads(query_part),
                split_heads(key_part),
                preferred_element_type=jnp.float32,
            )
            * score_scale
        )

    rows_f = own_rows.astype(jnp.float32)
    normed, inverse_in = normalize(rows_f)
    normed_bf = normed.astype(jnp.bfloat16)
    pre = jnp.dot(normed_bf, proj_weight, preferred_element_type=jnp.float32)
    proj = (pre * jax.nn.sigmoid(pre)).astype(jnp.bfloat16)
    update_rows = proj[:, :model_width]
    value_rows = proj[:, model_width : 2 * model_width]
    query_rows = proj[:, 2 * model_width : 3 * model_width]
    key_rows = proj[:, 3 * model_width :]

    def attend_block(running, pieces, first_row):
        key_part, value_part = pieces
        key_pos = position_of(first_row + jnp.arange(key_part.shape[0], dtype=jnp.int32))
        allowed = allowed_of(own_pos, own_users, key_pos, user_of(key_pos))[None]
        scores = piece_scores(query_rows, key_part)
        weights = jnp.where(allowed, scores * jax.nn.sigmoid(scores), 0.0).astype(jnp.bfloat16)
        product = jnp.einsum(
            "hqk,khd->qhd", weights, split_heads(value_part), preferred_element_type=jnp.float32
        )
        return running + merge_heads(product)

    zeros_rows = jnp.zeros((row_count, model_width), jnp.float32)
    attended = in_blocks(
        attend_block,
        row_count,
        zeros_rows,
        (
            lax.all_gather(key_rows, "ctx", axis=0, tiled=True),
            lax.all_gather(value_rows, "ctx", axis=0, tiled=True),
        ),
    )
    att_normed, inverse_att = normalize(attended)
    update_f = update_rows.astype(jnp.float32)
    gated = (att_normed * update_f).astype(jnp.bfloat16)
    layer_rows = (rows_f + jnp.dot(gated, out_weight, preferred_element_type=jnp.float32)).astype(
        jnp.bfloat16
    )
    out_term = jnp.dot(gated.T, cotangent, preferred_element_type=jnp.float32)
    grad_gated = jnp.dot(cotangent, out_weight.T, preferred_element_type=jnp.float32)
    grad_update = grad_gated * att_normed
    grad_att = normalize_back(grad_gated * update_f, att_normed, inverse_att).astype(jnp.bfloat16)

    def query_block(running, pieces, first_row):
        key_part, value_part = pieces
        key_pos = position_of(first_row + jnp.arange(key_part.shape[0], dtype=jnp.int32))
        allowed = allowed_of(own_pos, own_users, key_pos, user_of(key_pos))[None]
        scores = piece_scores(query_rows, key_part)
        grad_weights = jnp.einsum(
            "qhd,khd->hqk",
            split_heads(grad_att),
            split_heads(value_part),
            preferred_element_type=jnp.float32,
        )
        grad_scores = jnp.where(
            allowed, grad_weights * silu_grad(scores) * score_scale, 0.0
        ).astype(jnp.bfloat16)
        product = jnp.einsum(
            "hqk,khd->qhd", grad_scores, split_heads(key_part), preferred_element_type=jnp.float32
        )
        return running + merge_heads(product)

    def key_block(running, pieces, first_row):
        query_part, grad_part = pieces
        query_pos = position_of(first_row + jnp.arange(query_part.shape[0], dtype=jnp.int32))
        allowed = allowed_of(query_pos, user_of(query_pos), own_pos, own_users)[None]
        scores = piece_scores(query_part, key_rows)
        weights = jnp.where(allowed, scores * jax.nn.sigmoid(scores), 0.0).astype(jnp.bfloat16)
        grad_weights = jnp.einsum(
            "qhd,khd->hqk",
            split_heads(grad_part),
            split_heads(value_rows),
            preferred_element_type=jnp.float32,
        )
        grad_scores = jnp.where(
            allowed, grad_weights * silu_grad(scores) * score_scale, 0.0
        ).astype(jnp.bfloat16)
        grad_key = jnp.einsum(
            "hqk,qhd->khd", grad_scores, split_heads(query_part), preferred_element_type=jnp.float32
        )
        grad_value = jnp.einsum(
            "hqk,qhd->khd", weights, split_heads(grad_part), preferred_element_type=jnp.float32
        )
        return (running[0] + merge_heads(grad_key), running[1] + merge_heads(grad_value))

    grad_query = in_blocks(
        query_block,
        row_count,
        zeros_rows,
        (
            lax.all_gather(key_rows, "ctx", axis=0, tiled=True),
            lax.all_gather(value_rows, "ctx", axis=0, tiled=True),
        ),
    )
    grad_key, grad_value = in_blocks(
        key_block,
        row_count,
        (zeros_rows, zeros_rows),
        (
            lax.all_gather(query_rows, "ctx", axis=0, tiled=True),
            lax.all_gather(grad_att, "ctx", axis=0, tiled=True),
        ),
    )
    grad_proj = jnp.concatenate([grad_update, grad_value, grad_query, grad_key], axis=1)
    grad_pre = (grad_proj * silu_grad(pre)).astype(jnp.bfloat16)
    proj_term = jnp.dot(normed_bf.T, grad_pre, preferred_element_type=jnp.float32)
    grad_normed = jnp.dot(grad_pre, proj_weight.T, preferred_element_type=jnp.float32)
    row_grads = (
        cotangent.astype(jnp.float32) + normalize_back(grad_normed, normed, inverse_in)
    ).astype(jnp.bfloat16)
    proj_sum, out_sum = lax.psum((proj_term, out_term), ("dp", "ctx"))
    grad_scale = (row_count * device_count) ** (-0.5)
    return (layer_rows, row_grads, proj_sum * grad_scale, out_sum * grad_scale)


def solution(mesh):
    placed = (
        P(("dp", "ctx"), None),
        P(("dp", "ctx")),
        P(("dp", "ctx")),
        P("dp", None),
        P(),
        P(),
        P(("dp", "ctx"), None),
    )
    return jax.shard_map(
        local,
        mesh=mesh,
        in_specs=placed,
        out_specs=(P(("dp", "ctx"), None), P(("dp", "ctx"), None), P(), P()),
        check_vma=False,
    )
```

profile of v0, /device:TPU:1, one launch (start us, length us, event | category | flops | bytes accessed | tf_op | source)
XLA Modules:
  0.0 588.2 jit_solution(1761363450948704301)
XLA Ops:
  11.1 11.5 %all-to-all-start = ((bf16[128,3,512]{2,1,0:T(4,128)(2,1)}), bf16[128,3,512]{2,1,0:T(4,128)(2,1)S(1)}, u32[]{:S(2)}, u32[]{:S(2)}) async-start(bf16[128,3,512]{2,1,0:T(4,128)(2,1)} %reshape.616), calls=%async_computation | async-start | bytes 1048576 | tf_op jit(solution)/shard_map/all_to_all | solution.py:57
  22.7 13.9 %all-to-all-done = bf16[128,3,512]{2,1,0:T(4,128)(2,1)S(1)} async-done(((bf16[128,3,512]{2,1,0:T(4,128)(2,1)}), bf16[128,3,512]{2,1,0:T(4,128)(2,1)S(1)}, u32[]{:S(2)}, u32[]{:S(2)}) %all-to-all-start) | async-done | bytes 393248 | tf_op jit(solution)/shard_map/all_to_all | solution.py:57
  48.1 43.7 %all-gather.5.cloned.1.call-done = bf16[2048,512]{1,0:T(8,128)(2,1)} async-done(((bf16[256,512]{1,0:T(8,128)(2,1)}), bf16[2048,512]{1,0:T(8,128)(2,1)}) %all-gather.5.cloned.1.call-update) | async-done | bytes 2097168 | tf_op jit(solution)/shard_map/all_gather | solution.py:135
  91.8 4.0 copy.48
  95.7 50.7 %all-gather.7.cloned.1.call-done = bf16[2048,512]{1,0:T(8,128)(2,1)} async-done(((bf16[256,512]{1,0:T(8,128)(2,1)}), bf16[2048,512]{1,0:T(8,128)(2,1)}) %all-gather.7.cloned.1.call-update) | async-done | bytes 2097168 | tf_op jit(solution)/shard_map/all_gather | solution.py:134
  146.5 4.0 copy.49
  150.4 35.0 %while.50 = (s32[]{:T(128)}, f32[256,512]{0,1:T(8,128)S(1)}, bf16[2048,512]{0,1:T(8,128)(2,1)}, s32[256]{0:T(256)S(1)}, s32[4]{0:T(128)S(1)}, /*index=5*/bf16[20...) while((s32[]{:T(128)}, f32[256,512]{0,1:T(8,128)S(1)}, ...), condition=%wide.region_7.8_spmd.clone, body=%wide.region_5.7_spmd.clone.sunk | while | flops 138364160 | bytes 4071625 | solution.py:37
  178.7 2.2 fusion.118
  190.9 93.5 %while.52 = (s32[]{:T(128)}, f32[256,512]{0,1:T(8,128)}, bf16[2048,512]{0,1:T(8,128)(2,1)}, s32[256]{0:T(256)S(1)}, s32[4]{0:T(128)S(1)}, /*index=5*/bf16[2048,5...) while((s32[]{:T(128)}, f32[256,512]{0,1:T(8,128)}, ...), condition=%wide.region_17.18_spmd.clone, body=%wide.region_15.17_spmd.clone.sunk | while | flops 208094464 | bytes 12984529 | solution.py:37
  192.2 3.3 fusion.133
  195.5 2.9 copy.73
  198.4 2.3 fusion.134
  203.0 3.3 fusion.133
  206.3 2.9 copy.73
  209.2 2.4 fusion.134
  214.8 3.3 fusion.133
  218.1 2.9 copy.73
  221.0 2.4 fusion.134
  226.6 3.3 fusion.133
  229.9 2.9 copy.73
  232.8 2.5 fusion.134
  238.6 3.3 fusion.133
  241.9 2.9 copy.73
  244.8 2.3 fusion.134
  250.4 3.3 fusion.133
  253.7 2.9 copy.73
  256.6 2.3 fusion.134
  262.2 3.3 fusion.133
  265.4 2.9 copy.73
  268.3 2.3 fusion.134
  273.9 3.3 fusion.133
  277.2 2.9 copy.73
  280.1 2.3 fusion.134
  286.5 2.3 fusion.70
  288.8 123.4 %while.51 = (s32[]{:T(128)}, f32[256,512]{0,1:T(8,128)S(1)}, f32[256,512]{0,1:T(8,128)}, bf16[2048,512]{1,0:T(8,128)(2,1)}, s32[4]{0:T(128)S(1)}, /*index=5*/s32...) while((s32[]{:T(128)}, f32[256,512]{0,1:T(8,128)S(1)}, ...), condition=%wide.region_14.15_spmd.clone, body=%wide.region_12.14_spmd.clone.sunk | while | flops 279135488 | bytes 18555156 | solution.py:37
  289.9 2.8 fusion.125
  294.8 3.8 fusion.127
  298.6 3.3 fusion.126
  305.4 2.8 fusion.125
  310.2 3.8 fusion.127
  314.0 3.3 fusion.126
  320.8 2.8 fusion.125
  325.6 3.8 fusion.127
  329.4 3.3 fusion.126
  336.2 2.8 fusion.125
  341.0 3.8 fusion.127
  344.8 3.3 fusion.126
  351.6 2.8 fusion.125
  356.4 3.8 fusion.127
  360.2 3.3 fusion.126
  367.0 2.8 fusion.125
  371.9 3.8 fusion.127
  375.7 3.3 fusion.126
  382.4 2.8 fusion.125
  387.3 3.8 fusion.127
  391.1 3.3 fusion.126
  397.9 2.8 fusion.125
  402.7 3.8 fusion.127
  406.5 3.3 fusion.126
  415.2 3.0 fusion.45
  418.2 2.9 fusion.63
  421.1 2.1 fusion.46
  425.1 150.4 %all-reduce.3.cloned.1.call-done = (f32[512,2048]{1,0:T(8,128)}, f32[512,512]{1,0:T(8,128)}) async-done(((f32[512,2048]{1,0:T(8,128)}, f32[512,512]{1,0:T(8,128)}), (f32[512,2048]{1,0:T(8,128)}, f32[512,512]{1,0:T(8,128)})) %all-reduce.3.cloned.1.call-update) | async-done | bytes 5242896 | tf_op jit(solution)/shard_map/psum | solution.py:216
  575.6 5.0 broadcast_multiply_fusion
  (261 shorter events, 130.3 us)
Async XLA Ops:
  7.2 31.3 %copy-start = (bf16[512,2048]{1,0:T(8,128)(2,1)S(1)}, bf16[512,2048]{1,0:T(8,128)(2,1)}, u32[]{:S(2)}) copy-start(bf16[512,2048]{1,0:T(8,128)(2,1)} %param.17) | copy-start | bytes 6291460
  7.2 15.4 %copy-start.9 = (s32[256]{0:T(256)S(1)}, s32[256]{0:T(256)}, u32[]{:S(2)}) copy-start(s32[256]{0:T(256)} %param.15) | copy-start | bytes 3076
  11.1 25.5 %all-to-all-start = ((bf16[128,3,512]{2,1,0:T(4,128)(2,1)}), bf16[128,3,512]{2,1,0:T(4,128)(2,1)S(1)}, u32[]{:S(2)}, u32[]{:S(2)}) async-start(bf16[128,3,512]{2,1,0:T(4,128)(2,1)} %reshape.616), calls=%async_computation | async-start | bytes 1048576 | tf_op jit(solution)/shard_map/all_to_all | solution.py:57
  22.6 69.2 %all-gather.5.cloned.1.call-start = ((), (), s32[]{:S(2)}) async-start(), calls=%async_computation.1 | async-start | bytes 2359296 | tf_op jit(solution)/shard_map/all_gather | solution.py:135
  40.6 1.0 copy-start.7
  40.6 2.7 copy-start.10
  42.4 5.6 copy-start.5
  42.4 104.1 %all-gather.7.cloned.1.call-start = ((), (), s32[]{:S(2)}) async-start(), calls=%async_computation.2 | async-start | bytes 2359296 | tf_op jit(solution)/shard_map/all_gather | solution.py:134
  43.2 245.7 %all-gather.9.cloned.1.call-start = ((), (), s32[]{:S(2)}) async-start(), calls=%async_computation.3 | async-start | bytes 2359296 | tf_op jit(solution)/shard_map/all_gather | solution.py:205
  48.0 240.8 %all-gather.11.cloned.1.call-start = ((), (), s32[]{:S(2)}) async-start(), calls=%async_computation.4 | async-start | bytes 2359296 | tf_op jit(solution)/shard_map/all_gather | solution.py:206
  189.8 0.8 copy-start.4
  190.6 384.9 %all-reduce.3.cloned.1.call-start = ((), (), s32[]{:S(2)}) async-start(), calls=%async_computation.5 | async-start | bytes 10485760 | tf_op jit(solution)/shard_map/psum | solution.py:216
  284.4 4.4 copy-start.1
  298.6 3.3 copy-start.2
  303.4 0.8 copy-start.3
  314.0 3.3 copy-start.2
  318.8 0.8 copy-start.3
  329.4 3.3 copy-start.2
  334.2 0.8 copy-start.3
  344.8 3.3 copy-start.2
  349.7 0.8 copy-start.3
  360.2 3.3 copy-start.2
  365.1 0.8 copy-start.3
  375.7 3.3 copy-start.2
  380.5 0.8 copy-start.3
  391.1 3.3 copy-start.2
  395.9 0.8 copy-start.3
  406.5 3.3 copy-start.2
  411.3 0.8 copy-start.3
  423.2 0.9 copy-start.6
  575.6 5.0 copy-start.8
Sparse Core Ops, SparseCore 0:
  42.5 49.1 all-gather.4
  94.7 51.7 all-gather.6
  148.8 51.7 all-gather.8
  202.9 51.6 all-gather.10
  421.2 154.3 all-reduce.2
where the time goes:
time: 592 us; the launch traced here: 588 us
  waiting for transfers between devices  260 us (44%)
  matrix products  153 us (26%)
  local copies, waits for them, and re-layouts  101 us (17%)
  other arithmetic  47.6 us (8%)
  between operations  14 us (2%)
  starting transfers between devices  11.9 us (2%)
    psum x1, waiting for transfers between devices, local(): proj_sum, out_sum = lax.psum((proj_term, out_term), ('dp', 'ctx'))  150 us
    all_gather x1, waiting for transfers between devices, local(): lax.all_gather(key_rows, 'ctx', axis=0, tiled=True)  50.7 us
    dot_general x16, matrix products, piece_scores(): jnp.einsum('qhd,khd->hqk', split_heads(query_part), split_heads(key_part)...  48.4 us
    dynamic_slice x48, local copies, waits for them, and re-layouts, one_block(): lax.dynamic_slice_in_dim(each, start, block_rows, 0)  46.8 us
    all_gather x1, waiting for transfers between devices, local(): lax.all_gather(value_rows, 'ctx', axis=0, tiled=True)  43.7 us
    dot_general x8, matrix products, key_block(): jnp.einsum('hqk,qhd->khd', grad_scores, split_heads(query_part), preferre...  30.4 us
    dot_general x8, matrix products, key_block(): jnp.einsum('hqk,qhd->khd', weights, split_heads(grad_part), preferred_ele...  26.2 us
    mul x8, local copies, waits for them, and re-layouts, silu_grad(): return sigma * (1.0 + values * (1.0 - sigma))  23.1 us
  transfers between devices with their start and end apart: 6, of which 4 were waited for; matrix products, arithmetic and copies ran while one was open for 26% of the time, Pallas kernels for 0%

commit v1 on v0

v1 whole, which is shorter than its diff:
```python
import functools

import jax
import jax.numpy as jnp
from jax import lax
from jax.experimental import pallas as pl
from jax.experimental.pallas import tpu as pltpu
from jax.sharding import PartitionSpec as P

MESH = pl.DeviceIdType.MESH
F32 = jnp.float32
BF16 = jnp.bfloat16
norm_eps = 1e-05
VMEM_LIMIT = 48 * 2**20

NCTX = 8
HALF = 128
BLK = 256
NB = 8
WIDTH = 512
HD = 64
EVENTS = 2048
TILES = 640
UNITS = 5
ORDERS = ("zxy", "zxy", "xyz", "xyz", "yzx")


def normalize(values):
    centre = values - jnp.mean(values, axis=-1, keepdims=True)
    inverse = lax.rsqrt(jnp.mean(centre * centre, axis=-1, keepdims=True) + norm_eps)
    return (centre * inverse, inverse)


def normalize_back(grad_in, normed, inverse):
    mean_grad = jnp.mean(grad_in, axis=-1, keepdims=True)
    mean_cross = jnp.mean(grad_in * normed, axis=-1, keepdims=True)
    return (grad_in - mean_grad - normed * mean_cross) * inverse


def silu(z):
    h = 0.5 * z
    return h + h * jnp.tanh(h)


def silu_grad(z):
    h = 0.5 * z
    u = 1.0 + jnp.tanh(h)
    return 0.5 * (u + h * u * (2.0 - u))


def dot(a, b):
    return lax.dot_general(a, b, (((1,), (0,)), ((), ())), preferred_element_type=F32)


def dot_nt(a, b):
    return lax.dot_general(a, b, (((1,), (1,)), ((), ())), preferred_element_type=F32)


def low(a, b):
    return jnp.concatenate([a[:, :HD], b[:, :HD]], axis=1)


def high(a, b):
    return jnp.concatenate([a[:, HD:], b[:, HD:]], axis=1)


def mod(a, n):
    return lax.rem(a + n, n)


def third(a):
    return (a * 21846) >> 16


def ctx_barrier():
    cx = lax.axis_index("ctx")
    dp = lax.axis_index("dp")
    sem = pltpu.get_barrier_semaphore()
    for rel in range(1, NCTX):
        pl.semaphore_signal(
            sem, inc=1, device_id=(dp, lax.rem(cx + rel, NCTX)), device_id_type=MESH
        )
    pl.semaphore_wait(sem, NCTX - 1)


def arrive_kernel(
    rows_ref, sslot_ref, aslot_ref, w_ref,
    own_ref, normed_ref, upd_ref, qk_ref, v_ref,
    out, recv, qk_msg, v_msg, row_sems, send_sems, recv_sems, local_sems,
):
    dp, cx = lax.axis_index("dp"), lax.axis_index("ctx")
    me = dp * NCTX + cx
    ndev = 128

    rows = rows_ref[...]
    rows4 = jnp.concatenate([rows[:, q * 128 : q * 128 + 128] for q in range(4)], axis=0)
    slot = sslot_ref[...]
    to = third(slot)
    place = ((to - me) & (ndev - 1)) * 16 + (slot - 3 * to)
    target = jnp.concatenate([place + 4 * q for q in range(4)], axis=1)
    seen = lax.broadcasted_iota(jnp.int32, (BLK, 1024), 0)

    def pack(n, carry):
        hot = jnp.where(seen == target - n * BLK, 1.0, 0.0).astype(BF16)
        part = dot(hot, rows4).astype(BF16)
        out[pl.ds(n * 16, 16)] = part.reshape(16, 16, 128)

        def send(rel, carry):
            @pl.when(rel > 0)
            def _():
                d = lax.rem(me + rel, ndev)
                pltpu.make_async_remote_copy(
                    src_ref=out.at[rel],
                    dst_ref=recv.at[rel],
                    send_sem=row_sems.at[0],
                    recv_sem=row_sems.at[1],
                    device_id=(d // NCTX, lax.rem(d, NCTX)),
                    device_id_type=MESH,
                ).start()

            return carry

        return lax.fori_loop(n * 16, n * 16 + 16, send, carry)

    lax.fori_loop(0, 8, pack, 0)
    recv[0] = out[0]
    all_rows = pltpu.make_async_remote_copy(
        src_ref=out.at[pl.ds(1, ndev - 1)],
        dst_ref=recv.at[pl.ds(1, ndev - 1)],
        send_sem=row_sems.at[0],
        recv_sem=row_sems.at[1],
        device_id=(dp, cx),
        device_id_type=MESH,
    )
    aslot = jnp.transpose(jnp.broadcast_to(aslot_ref[...], (128, BLK)))[:, :1]
    come = third(aslot)
    picked = ((me - come) & (ndev - 1)) * 16 + (aslot - 3 * come)
    lanes = lax.broadcasted_iota(jnp.int32, (BLK, EVENTS), 1)
    all_rows.wait()

    got = recv[...].reshape(EVENTS, 128)
    own = jnp.concatenate(
        [
            dot(jnp.where(lanes == picked + 4 * q, 1.0, 0.0).astype(BF16), got)
            for q in range(4)
        ],
        axis=1,
    )
    own_ref[...] = own.astype(BF16)
    normed = normalize(own)[0].astype(BF16)
    normed_ref[...] = normed

    query = (silu(dot(normed, w_ref[:, 1024:1536])).astype(BF16).astype(F32) * 0.0625).astype(BF16)
    key = silu(dot(normed, w_ref[:, 1536:2048])).astype(BF16)
    for a in range(4):
        x, y = query[:, a * 128 : a * 128 + 128], key[:, a * 128 : a * 128 + 128]
        qk_msg[2 * a] = low(x, y).reshape(2, HALF, 128)
        qk_msg[2 * a + 1] = high(x, y).reshape(2, HALF, 128)

    def to_head(peer, rel, n):
        if n < 2:
            src, dst = qk_msg.at[peer, n], qk_ref.at[cx if n == 0 else 15 - cx]
        else:
            src, dst = v_msg.at[peer], v_ref.at[cx]
        if rel == 0:
            return pltpu.make_async_copy(src, dst, local_sems.at[n])
        return pltpu.make_async_remote_copy(
            src_ref=src,
            dst_ref=dst,
            send_sem=send_sems.at[rel, n],
            recv_sem=recv_sems.at[rel, n],
            device_id=(dp, peer),
            device_id_type=MESH,
        )

    copies = []
    for rel in range(NCTX):
        peer = lax.rem(cx + rel, NCTX)
        for n in range(2):
            copies.append(to_head(peer, rel, n))
            copies[-1].start()

    value = silu(dot(normed, w_ref[:, 512:1024])).astype(BF16)
    for a in range(4):
        x = value[:HALF, a * 128 : a * 128 + 128]
        y = value[HALF:, a * 128 : a * 128 + 128]
        v_msg[2 * a] = low(x, y)
        v_msg[2 * a + 1] = high(x, y)
    for rel in range(NCTX):
        copies.append(to_head(lax.rem(cx + rel, NCTX), rel, 2))
        copies[-1].start()

    upd_ref[...] = silu(dot(normed, w_ref[:, :512])).astype(BF16)
    for copy in copies:
        copy.wait()


def timeline_ends(len_ref):
    ends, total = [], 0
    for n in range(4):
        total = total + len_ref[0, n]
        ends.append(total)
    return ends


def start_of(positions, ends):
    first = jnp.zeros_like(positions)
    for n in range(3):
        first = jnp.where(positions >= ends[n], ends[n], first)
    return first


def end_of(position, ends):
    last = ends[3]
    for n in (2, 1, 0):
        last = jnp.where(position < ends[n], ends[n], last)
    return last


def in_position_order(packed, dst):
    for c in range(NCTX):
        block = packed[c]
        dst[c * HALF : (c + 1) * HALF, :] = block[:, :HD]
        dst[(15 - c) * HALF : (16 - c) * HALF, :] = block[:, HD:]


def forward_kernel(len_ref, qk_ref, v_ref, att_ref, q, kt, v, att):
    ends = timeline_ends(len_ref)
    qk = qk_ref[...].reshape(EVENTS, 128)
    q[...] = qk[:, :HD]
    kt[...] = jnp.transpose(qk)[HD:, :]
    in_position_order(v_ref, v)

    for i in range(NB):
        row = i * BLK + lax.broadcasted_iota(jnp.int32, (BLK, 1), 0)
        first = start_of(row, ends)
        q_i = q[i * BLK : (i + 1) * BLK, :]

        def block(j, acc):
            at = pl.multiple_of(j * BLK, BLK)
            h = dot(q_i, kt[:, pl.ds(at, BLK)])
            w = h + h * jnp.tanh(h)
            t = at + lax.broadcasted_iota(jnp.int32, (BLK, BLK), 1)
            w = jnp.where((t >= first) & (t <= row), w, 0.0).astype(BF16)
            return acc + dot(w, v[pl.ds(at, BLK), :])

        lowest = start_of(jnp.int32(i * BLK), ends) >> 8
        att[i * BLK : (i + 1) * BLK, :] = lax.fori_loop(
            lowest, i + 1, block, jnp.zeros((BLK, HD), F32)
        ).astype(BF16)

    for c in range(NCTX):
        att_ref[c] = jnp.concatenate(
            [att[c * HALF : (c + 1) * HALF, :], att[(15 - c) * HALF : (16 - c) * HALF, :]], axis=1
        )


def backward_kernel(
    len_ref, qk_ref, v_ref, ga_ref, g_ref, q, qt, k, kt, v, ga, gat, gqt, gk, gv
):
    ends = timeline_ends(len_ref)
    qk = qk_ref[...].reshape(EVENTS, 128)
    q[...] = qk[:, :HD]
    k[...] = qk[:, HD:]
    qkt = jnp.transpose(qk)
    qt[...] = qkt[:HD]
    kt[...] = qkt[HD:]
    in_position_order(v_ref, v)
    in_position_order(ga_ref, ga)
    gat[...] = jnp.transpose(ga[...])
    gqt[...] = jnp.zeros_like(gqt)

    for j in range(NB):
        t = j * BLK + lax.broadcasted_iota(jnp.int32, (BLK, 1), 0)
        keys = slice(j * BLK, (j + 1) * BLK)
        k_j, kt_j, v_j = k[keys, :], kt[:, keys], v[keys, :]

        def block(i, carry):
            gk_j, gv_j = carry
            at = pl.multiple_of(i * BLK, BLK)
            rows = pl.ds(at, BLK)
            h = dot(k_j, qt[:, rows])
            u = 1.0 + jnp.tanh(h)
            w = h * u
            e = dot(v_j, gat[:, rows]) * (u + w * (2.0 - u))
            p = at + lax.broadcasted_iota(jnp.int32, (1, BLK), 1)
            ok = (t >= start_of(p, ends)) & (t <= p)
            w = jnp.where(ok, w, 0.0).astype(BF16)
            e = jnp.where(ok, e, 0.0).astype(BF16)
            gqt[:, rows] += dot(kt_j, e)
            return gk_j + dot(e, q[rows, :]), gv_j + dot(w, ga[rows, :])

        zero = jnp.zeros((BLK, HD), F32)
        highest = (end_of(jnp.int32(j * BLK + BLK - 1), ends) - 1) >> 8
        gk_j, gv_j = lax.fori_loop(j, highest + 1, block, (zero, zero))
        gk[keys, :] = gk_j.astype(BF16)
        gv[keys, :] = gv_j.astype(BF16)

    gq = jnp.transpose(gqt[...] * 0.0625).astype(BF16)
    for c in range(NCTX):
        a = slice(c * HALF, (c + 1) * HALF)
        b = slice((15 - c) * HALF, (16 - c) * HALF)
        g_ref[c, 0] = jnp.concatenate([gv[a, :], gv[b, :]], axis=1)
        g_ref[c, 1] = jnp.concatenate([gq[a, :], gq[b, :]], axis=1)
        g_ref[c, 2] = jnp.concatenate([gk[a, :], gk[b, :]], axis=1)


def exchange(src, dst, sems, base=0):
    dp, cx = lax.axis_index("dp"), lax.axis_index("ctx")
    copies = []
    for rel in range(NCTX):
        peer = lax.rem(cx + rel, NCTX)
        if rel == 0:
            copy = pltpu.make_async_copy(src.at[peer], dst.at[cx], sems.at[base])
        else:
            copy = pltpu.make_async_remote_copy(
                src_ref=src.at[peer],
                dst_ref=dst.at[cx],
                send_sem=sems.at[base + rel],
                recv_sem=sems.at[base + NCTX + rel],
                device_id=(dp, peer),
                device_id_type=MESH,
            )
        copy.start()
        copies.append(copy)
    return copies


def gather_heads(parts):
    first = [low(parts[2 * a], parts[2 * a + 1]) for a in range(4)]
    second = [high(parts[2 * a], parts[2 * a + 1]) for a in range(4)]
    return jnp.concatenate(
        [jnp.concatenate(first, axis=1), jnp.concatenate(second, axis=1)], axis=0
    )


def middle_kernel(
    att_ref, own_ref, upd_ref, cot_ref, wo_ref,
    layer_ref, gu_ref, outterm_ref, ga_ref,
    att_in, ga_msg, sems,
):
    ctx_barrier()
    copies = exchange(att_ref, att_in, sems)
    cot = cot_ref[...]
    wo = wo_ref[...]
    grad_gated = dot_nt(cot, wo)
    update = upd_ref[...].astype(F32)
    for copy in copies:
        copy.wait()
    attended = gather_heads([att_in[h].astype(F32) for h in range(NCTX)])
    att_normed, inverse = normalize(attended)
    grad_att = normalize_back(grad_gated * update, att_normed, inverse).astype(BF16)
    for a in range(4):
        x = grad_att[:HALF, a * 128 : a * 128 + 128]
        y = grad_att[HALF:, a * 128 : a * 128 + 128]
        ga_msg[2 * a] = low(x, y)
        ga_msg[2 * a + 1] = high(x, y)
    copies = exchange(ga_msg, ga_ref, sems, 2 * NCTX)
    gated = (att_normed * update).astype(BF16)
    layer_ref[...] = (own_ref[...].astype(F32) + dot(gated, wo)).astype(BF16)
    outterm_ref[...] = dot(jnp.transpose(gated), cot)
    gu_ref[...] = grad_gated * att_normed
    for copy in copies:
        copy.wait()


def final_kernel(
    g_ref, own_ref, normed_ref, w_ref, cot_ref, gu_ref, outterm_ref,
    rowgrad_ref, sum_ref,
    g_in, mine, first_in, b1, in1, b2, in2, in3, sems, core_sems, axis_sems,
):
    dp, cx = lax.axis_index("dp"), lax.axis_index("ctx")
    core, xlo, z = lax.rem(dp, 2), lax.rem(dp // 2, 2), dp // 4
    xhi, y = lax.rem(cx, 2), cx // 2
    place = {"x": xhi * 2 + xlo, "y": y, "z": z}
    sibling = (dp + 1 - 2 * core, cx)

    def along(axis, r):
        c = lax.rem(place[axis] + r, 4)
        if axis == "x":
            return c, (z * 4 + lax.rem(c, 2) * 2 + core, y * 2 + c // 2)
        if axis == "y":
            return c, (dp, c * 2 + xhi)
        return c, (c * 4 + xlo * 2 + core, cx)

    barrier = pltpu.get_barrier_semaphore()
    for rel in range(1, NCTX):
        pl.semaphore_signal(
            barrier, inc=1, device_id=(dp, lax.rem(cx + rel, NCTX)), device_id_type=MESH
        )
    for device in [sibling] + [along(axis, r)[1] for axis in "xyz" for r in (1, 2, 3)]:
        pl.semaphore_signal(barrier, inc=1, device_id=device, device_id_type=MESH)
    pl.semaphore_wait(barrier, NCTX - 1 + 10)

    def remote(src, dst, send_sem, recv_sem, device):
        copy = pltpu.make_async_remote_copy(
            src_ref=src, dst_ref=dst, send_sem=send_sem, recv_sem=recv_sem,
            device_id=device, device_id_type=MESH,
        )
        copy.start()
        return copy

    copies = exchange(g_ref, g_in, sems)

    own, cot = own_ref[...].astype(F32), cot_ref[...]
    normed, inverse = normalize(own)
    normed_bf = normed_ref[...]
    normed_t = jnp.transpose(normed_bf)

    def put(block, term):
        term = term.astype(BF16)
        for n in range(4):
            mine[pl.ds((block * 4 + n) * 32, 32)] = term[:, n * 128 : n * 128 + 128].reshape(
                32, 16, 128
            )

    grad_normed = jnp.zeros((BLK, WIDTH), F32)

    def block_grads(block, grad, total):
        columns = slice(block * WIDTH, (block + 1) * WIDTH)
        w = w_ref[:, columns]
        grad_pre = (grad * silu_grad(dot(normed_bf, w))).astype(BF16)
        put(block, dot(normed_t, grad_pre))
        return total + dot_nt(grad_pre, w)

    put(4, outterm_ref[...])
    grad_normed = block_grads(0, gu_ref[...], grad_normed)
    for copy in copies:
        copy.wait()
    for n in range(3):
        grad = gather_heads([g_in[h, n].astype(F32) for h in range(NCTX)])
        grad_normed = block_grads(n + 1, grad, grad_normed)

    half = UNITS * 64
    copies = [
        remote(
            mine.at[pl.ds((1 - core) * half + u * 64, 64)], first_in.at[pl.ds(u * 64, 64)],
            core_sems.at[0, u], core_sems.at[1, u], sibling,
        )
        for u in range(UNITS)
    ]
    rowgrad_ref[...] = (
        cot.astype(F32) + normalize_back(grad_normed, normed, inverse)
    ).astype(BF16)
    for copy in copies:
        copy.wait()

    def add(own_part, parts):
        total = own_part.astype(F32)
        for part in parts:
            total = total + part.astype(F32)
        return total.astype(BF16)

    for u in range(UNITS):
        at = pl.ds(u * 64, 64)
        first_in[at] = add(first_in[at], [mine[pl.ds(core * half + u * 64, 64)]])

    stages = ((first_in, 16, in1, b1), (b1, 4, in2, b2), (b2, 1, in3, None))
    base = [0] * UNITS
    for step, (src, size, landing, dst) in enumerate(stages):
        copies = []
        for u in range(UNITS):
            axis = ORDERS[u][step]
            for r in (1, 2, 3):
                c, device = along(axis, r)
                copies.append(
                    remote(
                        src.at[pl.ds((u * 4 + c) * size, size)],
                        landing.at[r - 1, pl.ds(u * size, size)],
                        axis_sems.at[0, step, u, r], axis_sems.at[1, step, u, r], device,
                    )
                )
        for copy in copies:
            copy.wait()
        for u in range(UNITS):
            c = place[ORDERS[u][step]]
            base[u] = base[u] + c * size
            total = add(
                src[pl.ds((u * 4 + c) * size, size)],
                [landing[r, pl.ds(u * size, size)] for r in range(3)],
            )
            if dst is None:
                sum_ref[pl.ds(core * half + u * 64 + base[u], size)] = total
            else:
                dst[pl.ds(u * size, size)] = total

    for step, size in ((2, 1), (1, 4), (0, 16)):
        copies = []
        for u in range(UNITS):
            axis = ORDERS[u][step]
            held = sum_ref.at[pl.ds(core * half + u * 64 + base[u], size)]
            for r in (1, 2, 3):
                copies.append(
                    remote(
                        held, held,
                        axis_sems.at[2, step, u, r], axis_sems.at[3, step, u, r], along(axis, r)[1],
                    )
                )
            base[u] = base[u] - place[axis] * size
        for copy in copies:
            copy.wait()
    copies = []
    for u in range(UNITS):
        held = sum_ref.at[pl.ds(core * half + u * 64, 64)]
        copies.append(remote(held, held, core_sems.at[2, u], core_sems.at[3, u], sibling))
    for copy in copies:
        copy.wait()


def spread_kernel(scale, sum_ref, proj_ref, out_ref):
    n = pl.program_id(0)

    def write(dst):
        for t in range(4):
            dst[:, t * 128 : t * 128 + 128] = (
                sum_ref[t * 32 : t * 32 + 32].reshape(WIDTH, 128).astype(F32) * scale
            )

    @pl.when(n < 4)
    def _():
        write(proj_ref)

    @pl.when(n == 4)
    def _():
        write(out_ref)


VM = pl.BlockSpec(memory_space=pltpu.VMEM)
SM = pl.BlockSpec(memory_space=pltpu.SMEM)


def shape(*dims, dtype=BF16):
    return jax.ShapeDtypeStruct(dims, dtype)


def params(**kw):
    return pltpu.CompilerParams(vmem_limit_bytes=VMEM_LIMIT, **kw)


def local(loader_rows, send_slot, arrive_slot, user_lengths, proj_weight, out_weight, cotangent):
    own, normed, update, qk, v = pl.pallas_call(
        arrive_kernel,
        name="arrive",
        out_shape=(
            shape(BLK, WIDTH), shape(BLK, WIDTH), shape(BLK, WIDTH),
            shape(16, HALF, 128), shape(NCTX, HALF, 128),
        ),
        in_specs=[VM] * 4,
        out_specs=(VM,) * 5,
        scratch_shapes=[
            pltpu.VMEM((128, 16, 128), BF16),
            pltpu.VMEM((128, 16, 128), BF16),
            pltpu.VMEM((NCTX, 2, HALF, 128), BF16),
            pltpu.VMEM((NCTX, HALF, 128), BF16),
            pltpu.SemaphoreType.DMA((2,)),
            pltpu.SemaphoreType.DMA((NCTX, 3)),
            pltpu.SemaphoreType.DMA((NCTX, 3)),
            pltpu.SemaphoreType.DMA((3,)),
        ],
        compiler_params=params(has_side_effects=True),
    )(loader_rows, send_slot.reshape(1, BLK), arrive_slot.reshape(1, BLK), proj_weight)

    att = pl.pallas_call(
        forward_kernel,
        name="attend",
        out_shape=shape(NCTX, HALF, 128),
        in_specs=[SM, VM, VM],
        out_specs=VM,
        scratch_shapes=[
            pltpu.VMEM((EVENTS, HD), BF16),
            pltpu.VMEM((HD, EVENTS), BF16),
            pltpu.VMEM((EVENTS, HD), BF16),
            pltpu.VMEM((EVENTS, HD), BF16),
        ],
        compiler_params=params(),
    )(user_lengths, qk, v)

    layer_out, grad_update, out_term, grad_att = pl.pallas_call(
        middle_kernel,
        name="middle",
        out_shape=(
            shape(BLK, WIDTH), shape(BLK, WIDTH, dtype=F32), shape(WIDTH, WIDTH, dtype=F32),
            shape(NCTX, HALF, 128),
        ),
        in_specs=[VM] * 5,
        out_specs=(VM,) * 4,
        scratch_shapes=[
            pltpu.VMEM((NCTX, HALF, 128), BF16),
            pltpu.VMEM((NCTX, HALF, 128), BF16),
            pltpu.SemaphoreType.DMA((4 * NCTX,)),
        ],
        compiler_params=params(collective_id=1, has_side_effects=True),
    )(att, own, update, cotangent, out_weight)

    grads = pl.pallas_call(
        backward_kernel,
        name="attend_back",
        out_shape=shape(NCTX, 3, HALF, 128),
        in_specs=[SM, VM, VM, VM],
        out_specs=VM,
        scratch_shapes=[
            pltpu.VMEM((EVENTS, HD), BF16),
            pltpu.VMEM((HD, EVENTS), BF16),
            pltpu.VMEM((EVENTS, HD), BF16),
            pltpu.VMEM((HD, EVENTS), BF16),
            pltpu.VMEM((EVENTS, HD), BF16),
            pltpu.VMEM((EVENTS, HD), BF16),
            pltpu.VMEM((HD, EVENTS), BF16),
            pltpu.VMEM((HD, EVENTS), F32),
            pltpu.VMEM((EVENTS, HD), BF16),
            pltpu.VMEM((EVENTS, HD), BF16),
        ],
        compiler_params=params(),
    )(user_lengths, qk, v, grad_att)

    row_grads, sums = pl.pallas_call(
        final_kernel,
        name="final",
        out_shape=(shape(BLK, WIDTH), shape(TILES, 16, 128)),
        in_specs=[VM] * 7,
        out_specs=(VM,) * 2,
        scratch_shapes=[
            pltpu.VMEM((NCTX, 3, HALF, 128), BF16),
            pltpu.VMEM((TILES, 16, 128), BF16),
            pltpu.VMEM((UNITS * 64, 16, 128), BF16),
            pltpu.VMEM((UNITS * 16, 16, 128), BF16),
            pltpu.VMEM((3, UNITS * 16, 16, 128), BF16),
            pltpu.VMEM((UNITS * 4, 16, 128), BF16),
            pltpu.VMEM((3, UNITS * 4, 16, 128), BF16),
            pltpu.VMEM((3, UNITS, 16, 128), BF16),
            pltpu.SemaphoreType.DMA((2 * NCTX,)),
            pltpu.SemaphoreType.DMA((4, UNITS)),
            pltpu.SemaphoreType.DMA((4, 3, UNITS, 4)),
        ],
        compiler_params=params(collective_id=2, has_side_effects=True),
    )(grads, own, normed, proj_weight, cotangent, grad_update, out_term)

    proj_grad, out_grad = pl.pallas_call(
        functools.partial(spread_kernel, (BLK * 128) ** (-0.5)),
        name="spread",
        grid=(5,),
        out_shape=(shape(WIDTH, 4 * WIDTH, dtype=F32), shape(WIDTH, WIDTH, dtype=F32)),
        in_specs=[pl.BlockSpec((TILES // 5, 16, 128), lambda n: (n, 0, 0))],
        out_specs=(
            pl.BlockSpec((WIDTH, WIDTH), lambda n: (0, jnp.minimum(n, 3))),
            pl.BlockSpec((WIDTH, WIDTH), lambda n: (0, 0)),
        ),
        compiler_params=params(),
    )(sums)
    return (layer_out, row_grads, proj_grad, out_grad)


def solution(mesh):
    placed = (
        P(("dp", "ctx"), None),
        P(("dp", "ctx")),
        P(("dp", "ctx")),
        P("dp", None),
        P(),
        P(),
        P(("dp", "ctx"), None),
    )
    return jax.shard_map(
        local,
        mesh=mesh,
        in_specs=placed,
        out_specs=(P(("dp", "ctx"), None), P(("dp", "ctx"), None), P(), P()),
        check_vma=False,
    )
```

time: 592 us -> 148 us (0.25)
  waiting for transfers between devices: 260 us -> 0 us
  matrix products: 153 us -> 0 us
  Pallas kernels: 0 us -> 139 us
  local copies, waits for them, and re-layouts: 101 us -> 7.85 us
  other arithmetic: 47.6 us -> 0 us
  between operations: 14 us -> 0.75 us
  starting transfers between devices: 11.9 us -> 0 us
    dot_general x54 -> x0, matrix products: 153 us -> none  [the longest x16 48.4 us: piece_scores(): jnp.einsum('qhd,khd->hqk', split_heads(query_part), split_heads(key_part)...]
    psum x1 -> x0, waiting for transfers between devices: 150 us -> none  [local(): proj_sum, out_sum = lax.psum((proj_term, out_term), ('dp', 'ctx'))]
    pallas_call x0 -> x6, Pallas kernels: none -> 139 us  [the longest x1 64.4 us: local(): pl.pallas_call(final_kernel, name='final', out_shape=(shape(BLK, WIDTH),...]
    all_gather x4 -> x0, waiting for transfers between devices: 94.4 us -> none  [the longest x1 50.7 us: local(): lax.all_gather(key_rows, 'ctx', axis=0, tiled=True)]
    dynamic_slice x48 -> x0, local copies, waits for them, and re-layouts: 46.8 us -> none  [one_block(): lax.dynamic_slice_in_dim(each, start, block_rows, 0)]
    add x24 -> x0, other arithmetic: 27.7 us -> none  [the longest x8 14.3 us: query_block(): return running + merge_heads(product)]
    mul x8 -> x0, local copies, waits for them, and re-layouts: 23.1 us -> none  [silu_grad(): return sigma * (1.0 + values * (1.0 - sigma))]
    all_to_all x1 -> x0, waiting for transfers between devices: 13.9 us -> none  [local(): lax.all_to_all(outgoing.reshape(device_count, capacity, model_width), ('d...]
  transfers between devices with their start and end apart: 6 -> 0, of which waited for: 4 -> 0; matrix products, arithmetic and copies ran while one was open for 26% -> 0% of each run, Pallas kernels for 0% -> 0%
where the time goes in v1:
time: 148 us; the launch traced here: 147 us
  Pallas kernels  139 us (94%)
  local copies, waits for them, and re-layouts  7.85 us (5%)
    pallas_call x1, Pallas kernels, local(): pl.pallas_call(final_kernel, name='final', out_shape=(shape(BLK, WIDTH),...  64.4 us
    pallas_call x1, Pallas kernels, local(): pl.pallas_call(arrive_kernel, name='arrive', out_shape=(shape(BLK, WIDTH)...  37.1 us
    pallas_call x1, Pallas kernels, local(): pl.pallas_call(middle_kernel, name='middle', out_shape=(shape(BLK, WIDTH)...  14 us
    pallas_call x1, Pallas kernels, local(): pl.pallas_call(backward_kernel, name='attend_back', out_shape=shape(NCTX,...  11.7 us
    pallas_call x1, Pallas kernels, local(): pl.pallas_call(forward_kernel, name='attend', out_shape=shape(NCTX, HALF,...  8 us
    unnamed x22, local copies, waits for them, and re-layouts  7.85 us
    pallas_call x1, Pallas kernels, local(): pl.pallas_call(functools.partial(spread_kernel, (BLK * 128) ** (-0.5)), n...  3.67 us

profile of v1, /device:TPU:1, one launch (start us, length us, event | category | flops | bytes accessed | tf_op | source)
XLA Modules:
  0.0 147.4 jit_solution(17705229863697329925)
XLA Ops:
  0.6 0.0 copy-start.7
  0.6 0.0 copy-start
  0.7 1.6 %copy-done = bf16[512,2048]{1,0:T(8,128)(2,1)S(1)} copy-done((bf16[512,2048]{1,0:T(8,128)(2,1)S(1)}, bf16[512,2048]{1,0:T(8,128)(2,1)}, u32[]{:S(2)}) %copy-start) | copy-done | bytes 2097176
  2.2 0.0 copy-start.5
  2.2 0.9 copy-done.5
  3.2 0.0 copy-start.8
  3.2 0.7 copy-done.8
  3.9 0.0 copy-start.9
  3.9 0.7 copy-done.9
  4.6 0.0 copy-start.3
  4.6 0.0 copy-start.4
  4.6 37.1 %arrive.1 = (bf16[256,512]{1,0:T(8,128)(2,1)S(1)}, bf16[256,512]{1,0:T(8,128)(2,1)S(1)}, bf16[256,512]{1,0:T(8,128)(2,1)S(1)}, bf16[16,128,128]{2,1,0:T(8,128)(2,1)S(1)}, bf16[8,128,128]{2,1,0:T(8,128)(2,1)S(1)}) custom-call(bf16[256,512]{1,0:T(8,128)(2,1)S(1)} %copy-done.5, s32[1,256]{1,0:T(1,128)S(1)} %bitcast.2, s32[1,256]{1,0:T(1,128)S(1)} %bitcast.3, ...), custom_call_target="tpu_custom_call" | custom-call | tf_op jit(solution)/shard_map/arrive/pallas_call | solution.py:541
  41.7 0.0 copy-start.1
  41.7 0.0 copy-start.6
  41.7 0.8 copy-done.6
  42.5 8.0 %attend.1.att_ref = bf16[8,128,128]{2,1,0:T(8,128)(2,1)S(1)} custom-call(s32[1,4]{1,0:T(1,128)S(1)} %copy-done.6, bf16[16,128,128]{2,1,0:T(8,128)(2,1)S(1)} %get-tuple-element.17.qk_ref, bf16[8,128,128]{2,1,0:T(8,128)(2,1)S(1)} %get-tuple-element.18.v_ref), custom_call_target="tpu_custom_call" | custom-call | tf_op jit(solution)/shard_map/attend/pallas_call | solution.py:563
  50.5 0.0 copy-done.3
  50.5 0.0 copy-done.4
  50.5 14.0 %middle.1 = (bf16[256,512]{1,0:T(8,128)(2,1)S(1)}, f32[256,512]{1,0:T(8,128)S(1)}, f32[512,512]{1,0:T(8,128)S(1)}, bf16[8,128,128]{2,1,0:T(8,128)(2,1)S(1)}) custom-call(bf16[8,128,128]{2,1,0:T(8,128)(2,1)S(1)} %attend.1.att_ref, bf16[256,512]{1,0:T(8,128)(2,1)S(1)} %get-tuple-element.19.own_ref, bf16[256,512]{1,0:T(8,128)(2,1)S(1)} %get-tuple-element.20.upd_ref, ...), custom_call_target="tpu_custom_call" | custom-call | tf_op jit(solution)/shard_map/middle/pallas_call | solution.py:578
  64.5 0.0 copy-done.7
  64.5 11.7 %attend_back.1.g_ref = bf16[8,3,128,128]{3,2,1,0:T(8,128)(2,1)S(1)} custom-call(s32[1,4]{1,0:T(1,128)S(1)} %copy-done.7, bf16[16,128,128]{2,1,0:T(8,128)(2,1)S(1)} %get-tuple-element.17.qk_ref, bf16[8,128,128]{2,1,0:T(8,128)(2,1)S(1)} %get-tuple-element.18.v_ref, bf16[8,128,128]{2,1,0:T(8,128)(2,1)S(1)} %get-tuple-element.22.ga_ref), custom_call_target="tpu_custom_call" | custom-call | tf_op jit(solution)/shard_map/attend_back/pallas_call | solution.py:595
  76.2 0.0 copy-done.1
  76.3 64.4 %final.1 = (bf16[256,512]{1,0:T(8,128)(2,1)S(1)}, bf16[640,16,128]{2,1,0:T(8,128)(2,1)}) custom-call(bf16[8,3,128,128]{3,2,1,0:T(8,128)(2,1)S(1)} %attend_back.1.g_ref, bf16[256,512]{1,0:T(8,128)(2,1)S(1)} %get-tuple-element.19.own_ref, bf16[256,512]{1,0:T(8,128)(2,1)S(1)} %get-tuple-element.23.normed_ref, bf16[512,2048]{1,0:T(8,128)(2,1)S(1)} %copy-done.1, ...), custom_call_target="tpu_custom_call" | custom-call | tf_op jit(solution)/shard_map/final/pallas_call | solution.py:616
  140.6 0.0 copy-start.2
  140.6 1.7 %copy-done.2 = bf16[640,16,128]{2,1,0:T(8,128)(2,1)S(1)} copy-done((bf16[640,16,128]{2,1,0:T(8,128)(2,1)S(1)}, bf16[640,16,128]{2,1,0:T(8,128)(2,1)}, u32[]{:S(2)}) %copy-start.2) | copy-done | bytes 2621464
  142.4 3.7 %spread.1 = (f32[512,2048]{1,0:T(8,128)}, f32[512,512]{1,0:T(8,128)}) custom-call(bf16[640,16,128]{2,1,0:T(8,128)(2,1)S(1)} %copy-done.2), custom_call_target="tpu_custom_call" | custom-call | tf_op jit(solution)/shard_map/spread/pallas_call | solution.py:638
  146.0 0.7 copy.13
  146.7 0.7 copy.14
Async XLA Ops:
  0.6 63.9 %copy-start.7 = (s32[1,4]{1,0:T(1,128)S(1)}, s32[1,4]{1,0:T(1,128)}, u32[]{:S(2)}) copy-start(s32[1,4]{1,0:T(1,128)} %len_ref.3) | copy-start | bytes 52
  0.6 1.6 %copy-start = (bf16[512,2048]{1,0:T(8,128)(2,1)S(1)}, bf16[512,2048]{1,0:T(8,128)(2,1)}, u32[]{:S(2)}) copy-start(bf16[512,2048]{1,0:T(8,128)(2,1)} %w_ref.3) | copy-start | bytes 6291460
  2.2 0.9 copy-start.5
  3.2 0.7 copy-start.8
  3.9 0.7 copy-start.9
  4.6 46.0 %copy-start.3 = (bf16[256,512]{1,0:T(8,128)(2,1)S(1)}, bf16[256,512]{1,0:T(8,128)(2,1)}, u32[]{:S(2)}) copy-start(bf16[256,512]{1,0:T(8,128)(2,1)} %cot_ref.3) | copy-start | bytes 786436
  4.6 46.0 %copy-start.4 = (bf16[512,512]{1,0:T(8,128)(2,1)S(1)}, bf16[512,512]{1,0:T(8,128)(2,1)}, u32[]{:S(2)}) copy-start(bf16[512,512]{1,0:T(8,128)(2,1)} %wo_ref.1) | copy-start | bytes 1572868
  41.7 34.6 %copy-start.1 = (bf16[512,2048]{1,0:T(8,128)(2,1)S(1)}, bf16[512,2048]{1,0:T(8,128)(2,1)}, u32[]{:S(2)}) copy-start(bf16[512,2048]{1,0:T(8,128)(2,1)} %w_ref.3) | copy-start | bytes 6291460
  41.7 0.8 copy-start.6
  140.6 1.7 %copy-start.2 = (bf16[640,16,128]{2,1,0:T(8,128)(2,1)S(1)}, bf16[640,16,128]{2,1,0:T(8,128)(2,1)}, u32[]{:S(2)}) copy-start(bf16[640,16,128]{2,1,0:T(8,128)(2,1)} %get-tuple-element.27.sum_ref) | copy-start | bytes 7864324

commit v2 on v1

--- a/solution.py
+++ b/solution.py
@@ -11,7 +11,7 @@
 F32 = jnp.float32
 BF16 = jnp.bfloat16
 norm_eps = 1e-05
-VMEM_LIMIT = 48 * 2**20
+VMEM_LIMIT = 32 * 2**20
 
 NCTX = 8
 HALF = 128
@@ -22,7 +22,7 @@
 EVENTS = 2048
 TILES = 640
 UNITS = 5
-ORDERS = ("zxy", "zxy", "xyz", "xyz", "yzx")
+ORDERS = ("zxy", "zyx", "xyz", "yzx", "zxy")
 
 
 def normalize(values):
@@ -72,7 +72,7 @@
     return (a * 21846) >> 16
 
 
-def ctx_barrier():
+def greet_ctx():
     cx = lax.axis_index("ctx")
     dp = lax.axis_index("dp")
     sem = pltpu.get_barrier_semaphore()
@@ -80,18 +80,41 @@
         pl.semaphore_signal(
             sem, inc=1, device_id=(dp, lax.rem(cx + rel, NCTX)), device_id_type=MESH
         )
-    pl.semaphore_wait(sem, NCTX - 1)
+    return sem
 
 
 def arrive_kernel(
+    rows_hbm, sslot_hbm, aslot_hbm, w_hbm,
+    own_ref, normed_ref, upd_ref, qk_ref, v_ref,
     rows_ref, sslot_ref, aslot_ref, w_ref,
-    own_ref, normed_ref, upd_ref, qk_ref, v_ref,
-    out, recv, qk_msg, v_msg, row_sems, send_sems, recv_sems, local_sems,
+    out, recv, hot_ref, qk_msg, v_msg, row_sems, send_sems, recv_sems, local_sems, in_sems,
 ):
     dp, cx = lax.axis_index("dp"), lax.axis_index("ctx")
     me = dp * NCTX + cx
     ndev = 128
-
+    loads = [
+        pltpu.make_async_copy(src, dst, in_sems.at[n])
+        for n, (src, dst) in enumerate(
+            ((rows_hbm, rows_ref), (sslot_hbm, sslot_ref), (aslot_hbm, aslot_ref), (w_hbm, w_ref))
+        )
+    ]
+    for load in loads:
+        load.start()
+
+    def device(rel):
+        d = lax.rem(me + rel, ndev)
+        return (d // NCTX, lax.rem(d, NCTX))
+
+    barrier = pltpu.get_barrier_semaphore()
+
+    def greet(rel, carry):
+        pl.semaphore_signal(barrier, inc=1, device_id=device(rel), device_id_type=MESH)
+        return carry
+
+    lax.fori_loop(1, ndev, greet, 0)
+
+    for load in loads[:3]:
+        load.wait()
     rows = rows_ref[...]
     rows4 = jnp.concatenate([rows[:, q * 128 : q * 128 + 128] for q in range(4)], axis=0)
     slot = sslot_ref[...]
@@ -104,25 +127,24 @@
         hot = jnp.where(seen == target - n * BLK, 1.0, 0.0).astype(BF16)
         part = dot(hot, rows4).astype(BF16)
         out[pl.ds(n * 16, 16)] = part.reshape(16, 16, 128)
-
-        def send(rel, carry):
-            @pl.when(rel > 0)
-            def _():
-                d = lax.rem(me + rel, ndev)
-                pltpu.make_async_remote_copy(
-                    src_ref=out.at[rel],
-                    dst_ref=recv.at[rel],
-                    send_sem=row_sems.at[0],
-                    recv_sem=row_sems.at[1],
-                    device_id=(d // NCTX, lax.rem(d, NCTX)),
-                    device_id_type=MESH,
-                ).start()
-
-            return carry
-
-        return lax.fori_loop(n * 16, n * 16 + 16, send, carry)
+        return carry
 
     lax.fori_loop(0, 8, pack, 0)
+
+    pl.semaphore_wait(barrier, ndev - 1)
+
+    def send(rel, carry):
+        pltpu.make_async_remote_copy(
+            src_ref=out.at[rel],
+            dst_ref=recv.at[rel],
+            send_sem=row_sems.at[0],
+            recv_sem=row_sems.at[1],
+            device_id=device(rel),
+            device_id_type=MESH,
+        ).start()
+        return carry
+
+    lax.fori_loop(1, ndev, send, 0)
     recv[0] = out[0]
     all_rows = pltpu.make_async_remote_copy(
         src_ref=out.at[pl.ds(1, ndev - 1)],
@@ -136,16 +158,13 @@
     come = third(aslot)
     picked = ((me - come) & (ndev - 1)) * 16 + (aslot - 3 * come)
     lanes = lax.broadcasted_iota(jnp.int32, (BLK, EVENTS), 1)
+    for q in range(4):
+        hot_ref[q] = jnp.where(lanes == picked + 4 * q, 1.0, 0.0).astype(BF16)
+    loads[3].wait()
     all_rows.wait()
 
     got = recv[...].reshape(EVENTS, 128)
-    own = jnp.concatenate(
-        [
-            dot(jnp.where(lanes == picked + 4 * q, 1.0, 0.0).astype(BF16), got)
-            for q in range(4)
-        ],
-        axis=1,
-    )
+    own = jnp.concatenate([dot(hot_ref[q], got) for q in range(4)], axis=1)
     own_ref[...] = own.astype(BF16)
     normed = normalize(own)[0].astype(BF16)
     normed_ref[...] = normed
@@ -335,12 +354,21 @@
 
 
 def middle_kernel(
-    att_ref, own_ref, upd_ref, cot_ref, wo_ref,
+    att_ref, own_ref, upd_ref, cot_hbm, wo_hbm,
     layer_ref, gu_ref, outterm_ref, ga_ref,
-    att_in, ga_msg, sems,
+    cot_ref, wo_ref, att_in, ga_msg, sems, in_sems,
 ):
-    ctx_barrier()
+    loads = [
+        pltpu.make_async_copy(cot_hbm, cot_ref, in_sems.at[0]),
+        pltpu.make_async_copy(wo_hbm, wo_ref, in_sems.at[1]),
+    ]
+    for load in loads:
+        load.start()
+    barrier = greet_ctx()
+    pl.semaphore_wait(barrier, NCTX - 1)
     copies = exchange(att_ref, att_in, sems)
+    for load in loads:
+        load.wait()
     cot = cot_ref[...]
     wo = wo_ref[...]
     grad_gated = dot_nt(cot, wo)
@@ -367,7 +395,7 @@
 def final_kernel(
     g_ref, own_ref, normed_ref, w_ref, cot_ref, gu_ref, outterm_ref,
     rowgrad_ref, sum_ref,
-    g_in, mine, first_in, b1, in1, b2, in2, in3, sems, core_sems, axis_sems,
+    g_in, slope, acc, mine, core_in, out1, in1, out2, in2, out3, in3, sems, core_sems, axis_sems,
 ):
     dp, cx = lax.axis_index("dp"), lax.axis_index("ctx")
     core, xlo, z = lax.rem(dp, 2), lax.rem(dp // 2, 2), dp // 4
@@ -383,14 +411,29 @@
             return c, (dp, c * 2 + xhi)
         return c, (c * 4 + xlo * 2 + core, cx)
 
-    barrier = pltpu.get_barrier_semaphore()
-    for rel in range(1, NCTX):
-        pl.semaphore_signal(
-            barrier, inc=1, device_id=(dp, lax.rem(cx + rel, NCTX)), device_id_type=MESH
-        )
+    barrier = greet_ctx()
     for device in [sibling] + [along(axis, r)[1] for axis in "xyz" for r in (1, 2, 3)]:
         pl.semaphore_signal(barrier, inc=1, device_id=device, device_id_type=MESH)
-    pl.semaphore_wait(barrier, NCTX - 1 + 10)
+
+    own, cot = own_ref[...].astype(F32), cot_ref[...]
+    normed, inverse = normalize(own)
+    normed_bf = normed_ref[...]
+    normed_t = jnp.transpose(normed_bf)
+
+    def put(u, term):
+        for n in range(4):
+            part = term[:, n * 128 : n * 128 + 128].reshape(32, 16, 128)
+            at = pl.ds(u * 64 + (n % 2) * 32, 32)
+            acc[n // 2, at] = part
+            mine[n // 2, at] = part.astype(BF16)
+
+    def columns(block):
+        return w_ref[:, block * WIDTH : (block + 1) * WIDTH]
+
+    def unit_grads(u, block, grad, slope):
+        grad_pre = (grad * slope).astype(BF16)
+        put(u, dot(normed_t, grad_pre))
+        return dot_nt(grad_pre, columns(block))
 
     def remote(src, dst, send_sem, recv_sem, device):
         copy = pltpu.make_async_remote_copy(
@@ -400,131 +443,159 @@
         copy.start()
         return copy
 
-    copies = exchange(g_ref, g_in, sems)
-
-    own, cot = own_ref[...].astype(F32), cot_ref[...]
-    normed, inverse = normalize(own)
-    normed_bf = normed_ref[...]
-    normed_t = jnp.transpose(normed_bf)
-
-    def put(block, term):
-        term = term.astype(BF16)
-        for n in range(4):
-            mine[pl.ds((block * 4 + n) * 32, 32)] = term[:, n * 128 : n * 128 + 128].reshape(
-                32, 16, 128
+    running = {}
+    lead = (out1, out2, out3)
+    landing = (in1, in2, in3)
+    sizes = (16, 4, 1)
+    base = [u * 64 for u in range(UNITS)]
+
+    def core_start(u):
+        at = pl.ds(u * 64, 64)
+        running[u] = [
+            remote(
+                mine.at[1 - core, at], core_in.at[at], core_sems.at[0, u], core_sems.at[1, u], sibling
             )
-
-    grad_normed = jnp.zeros((BLK, WIDTH), F32)
-
-    def block_grads(block, grad, total):
-        columns = slice(block * WIDTH, (block + 1) * WIDTH)
-        w = w_ref[:, columns]
-        grad_pre = (grad * silu_grad(dot(normed_bf, w))).astype(BF16)
-        put(block, dot(normed_t, grad_pre))
-        return total + dot_nt(grad_pre, w)
-
-    put(4, outterm_ref[...])
-    grad_normed = block_grads(0, gu_ref[...], grad_normed)
-    for copy in copies:
+        ]
+
+    def finish(u):
+        for copy in running.pop(u):
+            copy.wait()
+
+    def core_finish(u):
+        finish(u)
+        at = pl.ds(u * 64, 64)
+        total = acc[core, at] + core_in[at].astype(F32)
+        acc[core, at] = total
+        out1[at] = total.astype(BF16)
+
+    def axis_start(u, step):
+        size = sizes[step]
+        running[u] = []
+        for r in (1, 2, 3):
+            c, device = along(ORDERS[u][step], r)
+            running[u].append(
+                remote(
+                    lead[step].at[pl.ds((u * 4 + c) * size, size)],
+                    landing[step].at[r - 1, pl.ds(u * size, size)],
+                    axis_sems.at[0, step, u, r], axis_sems.at[1, step, u, r], device,
+                )
+            )
+
+    def axis_finish(u, step):
+        finish(u)
+        size = sizes[step]
+        base[u] = base[u] + place[ORDERS[u][step]] * size
+        total = acc[core, pl.ds(base[u], size)]
+        for r in range(3):
+            total = total + landing[step][r, pl.ds(u * size, size)].astype(F32)
+        if step == 2:
+            sum_ref[pl.ds(core * (UNITS * 64) + base[u], size)] = total.astype(BF16)
+        else:
+            acc[core, pl.ds(base[u], size)] = total
+            lead[step + 1][pl.ds(u * size, size)] = total.astype(BF16)
+
+    def back_start(u, step):
+        size = sizes[step]
+        held = sum_ref.at[pl.ds(core * (UNITS * 64) + base[u], size)]
+        axis = ORDERS[u][step]
+        running[u] = [
+            remote(
+                held, held, axis_sems.at[2, step, u, r], axis_sems.at[3, step, u, r], along(axis, r)[1]
+            )
+            for r in (1, 2, 3)
+        ]
+        base[u] = base[u] - place[axis] * size
+
+    def core_back(u):
+        held = sum_ref.at[pl.ds((core * UNITS + u) * 64, 64)]
+        running[u] = [remote(held, held, core_sems.at[2, u], core_sems.at[3, u], sibling)]
+
+    put(1, outterm_ref[...])
+    grad_normed = unit_grads(0, 0, gu_ref[...], silu_grad(dot(normed_bf, columns(0))))
+    pl.semaphore_wait(barrier, NCTX - 1 + 10)
+    g_copies = exchange(g_ref, g_in, sems)
+    early, late = (0, 1), (2, 3, 4)
+    for u in early:
+        core_start(u)
+    for n in range(3):
+        slope[n] = silu_grad(dot(normed_bf, columns(n + 1)))
+    for u in early:
+        core_finish(u)
+        axis_start(u, 0)
+    for copy in g_copies:
         copy.wait()
-    for n in range(3):
+    for n, u in enumerate(late):
         grad = gather_heads([g_in[h, n].astype(F32) for h in range(NCTX)])
-        grad_normed = block_grads(n + 1, grad, grad_normed)
-
-    half = UNITS * 64
-    copies = [
-        remote(
-            mine.at[pl.ds((1 - core) * half + u * 64, 64)], first_in.at[pl.ds(u * 64, 64)],
-            core_sems.at[0, u], core_sems.at[1, u], sibling,
-        )
-        for u in range(UNITS)
-    ]
+        grad_normed = grad_normed + unit_grads(u, n + 1, grad, slope[n])
+        core_start(u)
     rowgrad_ref[...] = (
         cot.astype(F32) + normalize_back(grad_normed, normed, inverse)
     ).astype(BF16)
+    for u in early:
+        axis_finish(u, 0)
+        axis_start(u, 1)
+    for u in late:
+        core_finish(u)
+        axis_start(u, 0)
+    for u in early:
+        axis_finish(u, 1)
+        axis_start(u, 2)
+    for u in late:
+        axis_finish(u, 0)
+        axis_start(u, 1)
+    for u in early:
+        axis_finish(u, 2)
+        back_start(u, 2)
+    for u in late:
+        axis_finish(u, 1)
+        axis_start(u, 2)
+    for u in early:
+        finish(u)
+        back_start(u, 1)
+    for u in late:
+        axis_finish(u, 2)
+        back_start(u, 2)
+    for u in early:
+        finish(u)
+        back_start(u, 0)
+    for u in late:
+        finish(u)
+        back_start(u, 1)
+    for u in early:
+        finish(u)
+        core_back(u)
+    for u in late:
+        finish(u)
+        back_start(u, 0)
+    for u in late:
+        finish(u)
+        core_back(u)
+    for u in early + late:
+        finish(u)
+
+
+def spread_kernel(scale, sum_ref, layer_ref, rowgrad_ref, proj_hbm, out_hbm, layer_hbm, rowgrad_hbm, wide, sems):
+    copies = [
+        pltpu.make_async_copy(layer_ref, layer_hbm, sems.at[5]),
+        pltpu.make_async_copy(rowgrad_ref, rowgrad_hbm, sems.at[6]),
+    ]
+    for copy in copies:
+        copy.start()
+    for u in range(UNITS):
+        for n in range(4):
+            at = (n // 2) * UNITS * 64 + u * 64 + (n % 2) * 32
+            wide[u, :, n * 128 : n * 128 + 128] = (
+                sum_ref[at : at + 32].reshape(WIDTH, 128).astype(F32) * scale
+            )
+        block = (0, None, 1, 2, 3)[u]
+        dst = out_hbm if block is None else proj_hbm.at[:, pl.ds(block * WIDTH, WIDTH)]
+        copies.append(pltpu.make_async_copy(wide.at[u], dst, sems.at[u]))
+        copies[-1].start()
     for copy in copies:
         copy.wait()
 
-    def add(own_part, parts):
-        total = own_part.astype(F32)
-        for part in parts:
-            total = total + part.astype(F32)
-        return total.astype(BF16)
-
-    for u in range(UNITS):
-        at = pl.ds(u * 64, 64)
-        first_in[at] = add(first_in[at], [mine[pl.ds(core * half + u * 64, 64)]])
-
-    stages = ((first_in, 16, in1, b1), (b1, 4, in2, b2), (b2, 1, in3, None))
-    base = [0] * UNITS
-    for step, (src, size, landing, dst) in enumerate(stages):
-        copies = []
-        for u in range(UNITS):
-            axis = ORDERS[u][step]
-            for r in (1, 2, 3):
-                c, device = along(axis, r)
-                copies.append(
-                    remote(
-                        src.at[pl.ds((u * 4 + c) * size, size)],
-                        landing.at[r - 1, pl.ds(u * size, size)],
-                        axis_sems.at[0, step, u, r], axis_sems.at[1, step, u, r], device,
-                    )
-                )
-        for copy in copies:
-            copy.wait()
-        for u in range(UNITS):
-            c = place[ORDERS[u][step]]
-            base[u] = base[u] + c * size
-            total = add(
-                src[pl.ds((u * 4 + c) * size, size)],
-                [landing[r, pl.ds(u * size, size)] for r in range(3)],
-            )
-            if dst is None:
-                sum_ref[pl.ds(core * half + u * 64 + base[u], size)] = total
-            else:
-                dst[pl.ds(u * size, size)] = total
-
-    for step, size in ((2, 1), (1, 4), (0, 16)):
-        copies = []
-        for u in range(UNITS):
-            axis = ORDERS[u][step]
-            held = sum_ref.at[pl.ds(core * half + u * 64 + base[u], size)]
-            for r in (1, 2, 3):
-                copies.append(
-                    remote(
-                        held, held,
-                        axis_sems.at[2, step, u, r], axis_sems.at[3, step, u, r], along(axis, r)[1],
-                    )
-                )
-            base[u] = base[u] - place[axis] * size
-        for copy in copies:
-            copy.wait()
-    copies = []
-    for u in range(UNITS):
-        held = sum_ref.at[pl.ds(core * half + u * 64, 64)]
-        copies.append(remote(held, held, core_sems.at[2, u], core_sems.at[3, u], sibling))
-    for copy in copies:
-        copy.wait()
-
-
-def spread_kernel(scale, sum_ref, proj_ref, out_ref):
-    n = pl.program_id(0)
-
-    def write(dst):
-        for t in range(4):
-            dst[:, t * 128 : t * 128 + 128] = (
-                sum_ref[t * 32 : t * 32 + 32].reshape(WIDTH, 128).astype(F32) * scale
-            )
-
-    @pl.when(n < 4)
-    def _():
-        write(proj_ref)
-
-    @pl.when(n == 4)
-    def _():
-        write(out_ref)
-
-
+
+HBM = pl.BlockSpec(memory_space=pltpu.HBM)
 VM = pl.BlockSpec(memory_space=pltpu.VMEM)
 SM = pl.BlockSpec(memory_space=pltpu.SMEM)
 
@@ -545,19 +616,25 @@
             shape(BLK, WIDTH), shape(BLK, WIDTH), shape(BLK, WIDTH),
             shape(16, HALF, 128), shape(NCTX, HALF, 128),
         ),
-        in_specs=[VM] * 4,
+        in_specs=[HBM] * 4,
         out_specs=(VM,) * 5,
         scratch_shapes=[
+            pltpu.VMEM((BLK, WIDTH), BF16),
+            pltpu.VMEM((1, BLK), jnp.int32),
+            pltpu.VMEM((1, BLK), jnp.int32),
+            pltpu.VMEM((WIDTH, 4 * WIDTH), BF16),
             pltpu.VMEM((128, 16, 128), BF16),
             pltpu.VMEM((128, 16, 128), BF16),
+            pltpu.VMEM((4, BLK, EVENTS), BF16),
             pltpu.VMEM((NCTX, 2, HALF, 128), BF16),
             pltpu.VMEM((NCTX, HALF, 128), BF16),
             pltpu.SemaphoreType.DMA((2,)),
             pltpu.SemaphoreType.DMA((NCTX, 3)),
             pltpu.SemaphoreType.DMA((NCTX, 3)),
             pltpu.SemaphoreType.DMA((3,)),
+            pltpu.SemaphoreType.DMA((4,)),
         ],
-        compiler_params=params(has_side_effects=True),
+        compiler_params=params(collective_id=0, has_side_effects=True),
     )(loader_rows, send_slot.reshape(1, BLK), arrive_slot.reshape(1, BLK), proj_weight)
 
     att = pl.pallas_call(
@@ -582,12 +659,15 @@
             shape(BLK, WIDTH), shape(BLK, WIDTH, dtype=F32), shape(WIDTH, WIDTH, dtype=F32),
             shape(NCTX, HALF, 128),
         ),
-        in_specs=[VM] * 5,
+        in_specs=[VM, VM, VM, HBM, HBM],
         out_specs=(VM,) * 4,
         scratch_shapes=[
+            pltpu.VMEM((BLK, WIDTH), BF16),
+            pltpu.VMEM((WIDTH, WIDTH), BF16),
             pltpu.VMEM((NCTX, HALF, 128), BF16),
             pltpu.VMEM((NCTX, HALF, 128), BF16),
             pltpu.SemaphoreType.DMA((4 * NCTX,)),
+            pltpu.SemaphoreType.DMA((2,)),
         ],
         compiler_params=params(collective_id=1, has_side_effects=True),
     )(att, own, update, cotangent, out_weight)
@@ -621,12 +701,15 @@
         out_specs=(VM,) * 2,
         scratch_shapes=[
             pltpu.VMEM((NCTX, 3, HALF, 128), BF16),
-            pltpu.VMEM((TILES, 16, 128), BF16),
+            pltpu.VMEM((3, BLK, WIDTH), F32),
+            pltpu.VMEM((2, UNITS * 64, 16, 128), F32),
+            pltpu.VMEM((2, UNITS * 64, 16, 128), BF16),
             pltpu.VMEM((UNITS * 64, 16, 128), BF16),
+            pltpu.VMEM((UNITS * 64, 16, 128), BF16),
+            pltpu.VMEM((3, UNITS * 16, 16, 128), BF16),
             pltpu.VMEM((UNITS * 16, 16, 128), BF16),
-            pltpu.VMEM((3, UNITS * 16, 16, 128), BF16),
+            pltpu.VMEM((3, UNITS * 4, 16, 128), BF16),
             pltpu.VMEM((UNITS * 4, 16, 128), BF16),
-            pltpu.VMEM((3, UNITS * 4, 16, 128), BF16),
             pltpu.VMEM((3, UNITS, 16, 128), BF16),
             pltpu.SemaphoreType.DMA((2 * NCTX,)),
             pltpu.SemaphoreType.DMA((4, UNITS)),
@@ -635,18 +718,21 @@
         compiler_params=params(collective_id=2, has_side_effects=True),
     )(grads, own, normed, proj_weight, cotangent, grad_update, out_term)
 
-    proj_grad, out_grad = pl.pallas_call(
+    proj_grad, out_grad, layer_out, row_grads = pl.pallas_call(
         functools.partial(spread_kernel, (BLK * 128) ** (-0.5)),
         name="spread",
-        grid=(5,),
-        out_shape=(shape(WIDTH, 4 * WIDTH, dtype=F32), shape(WIDTH, WIDTH, dtype=F32)),
-        in_specs=[pl.BlockSpec((TILES // 5, 16, 128), lambda n: (n, 0, 0))],
-        out_specs=(
-            pl.BlockSpec((WIDTH, WIDTH), lambda n: (0, jnp.minimum(n, 3))),
-            pl.BlockSpec((WIDTH, WIDTH), lambda n: (0, 0)),
+        out_shape=(
+            shape(WIDTH, 4 * WIDTH, dtype=F32), shape(WIDTH, WIDTH, dtype=F32),
+            shape(BLK, WIDTH), shape(BLK, WIDTH),
         ),
+        in_specs=[VM] * 3,
+        out_specs=(HBM,) * 4,
+        scratch_shapes=[
+            pltpu.VMEM((UNITS, WIDTH, WIDTH), F32),
+            pltpu.SemaphoreType.DMA((7,)),
+        ],
         compiler_params=params(),
-    )(sums)
+    )(sums, layer_out, row_grads)
     return (layer_out, row_grads, proj_grad, out_grad)
 
 

time: 148 us -> 129 us (0.87)
  Pallas kernels: 139 us -> 123 us
  local copies, waits for them, and re-layouts: 7.85 us -> 4.7 us
    pallas_call x1, Pallas kernels: 64.4 us -> 51.9 us  [local(): pl.pallas_call(final_kernel, name='final', out_shape=(shape(BLK, WIDTH),...]
    pallas_call x1, Pallas kernels: 37.1 us -> 33.7 us  [local(): pl.pallas_call(arrive_kernel, name='arrive', out_shape=(shape(BLK, WIDTH)...]
    unnamed x22 -> x16, local copies, waits for them, and re-layouts: 7.85 us -> 4.7 us
where the time goes in v2:
time: 129 us
  Pallas kernels  123 us (95%)
  local copies, waits for them, and re-layouts  4.7 us (4%)
    pallas_call x1, Pallas kernels, local(): pl.pallas_call(final_kernel, name='final', out_shape=(shape(BLK, WIDTH),...  51.9 us
    pallas_call x1, Pallas kernels, local(): pl.pallas_call(arrive_kernel, name='arrive', out_shape=(shape(BLK, WIDTH)...  33.7 us
    pallas_call x1, Pallas kernels, local(): pl.pallas_call(middle_kernel, name='middle', out_shape=(shape(BLK, WIDTH)...  14.4 us
    pallas_call x1, Pallas kernels, local(): pl.pallas_call(backward_kernel, name='attend_back', out_shape=shape(NCTX,...  12.3 us
    pallas_call x1, Pallas kernels, local(): pl.pallas_call(forward_kernel, name='attend', out_shape=shape(NCTX, HALF,...  8.32 us
    unnamed x16, local copies, waits for them, and re-layouts  4.7 us
    pallas_call x1, Pallas kernels, local(): pl.pallas_call(functools.partial(spread_kernel, (BLK * 128) ** (-0.5)), n...  2.59 us

profile of v2, /device:TPU:1, one launch (start us, length us, event | category | flops | bytes accessed | tf_op | source)
XLA Modules:
  0.0 128.8 jit_solution(6996844133391273907)
XLA Ops:
  0.6 0.0 copy-start
  0.6 1.6 %copy-done = bf16[512,2048]{1,0:T(8,128)(2,1)S(1)} copy-done((bf16[512,2048]{1,0:T(8,128)(2,1)S(1)}, bf16[512,2048]{1,0:T(8,128)(2,1)}, u32[]{:S(2)}) %copy-start) | copy-done | bytes 2097176
  2.2 0.0 copy-start.4
  2.2 0.9 copy-done.4
  3.2 0.0 copy-start.6
  3.2 0.7 copy-done.6
  3.9 0.0 copy-start.7
  3.9 0.7 copy-done.7
  4.5 0.0 copy-start.2
  4.5 0.0 copy-start.3
  4.5 33.7 %arrive.1 = (bf16[256,512]{1,0:T(8,128)(2,1)S(1)}, bf16[256,512]{1,0:T(8,128)(2,1)S(1)}, bf16[256,512]{1,0:T(8,128)(2,1)S(1)}, bf16[16,128,128]{2,1,0:T(8,128)(2,1)S(1)}, bf16[8,128,128]{2,1,0:T(8,128)(2,1)S(1)}) custom-call(bf16[256,512]{1,0:T(8,128)(2,1)S(1)} %copy-done.4, s32[1,256]{1,0:T(1,128)S(1)} %bitcast.2, s32[1,256]{1,0:T(1,128)S(1)} %bitcast.3, ...), custom_call_target="tpu_custom_call" | custom-call | tf_op jit(solution)/shard_map/arrive/pallas_call | solution.py:612
  38.3 0.0 copy-start.1
  38.3 0.0 copy-start.5
  38.3 0.8 copy-done.5
  39.1 8.3 %attend.1.att_ref = bf16[8,128,128]{2,1,0:T(8,128)(2,1)S(1)} custom-call(s32[1,4]{1,0:T(1,128)S(1)} %copy-done.5, bf16[16,128,128]{2,1,0:T(8,128)(2,1)S(1)} %get-tuple-element.19.qk_ref, bf16[8,128,128]{2,1,0:T(8,128)(2,1)S(1)} %get-tuple-element.20.v_ref), custom_call_target="tpu_custom_call" | custom-call | tf_op jit(solution)/shard_map/attend/pallas_call | solution.py:640
  47.4 0.0 copy-done.2
  47.4 0.0 copy-done.3
  47.4 14.4 %middle.1 = (bf16[256,512]{1,0:T(8,128)(2,1)S(1)}, f32[256,512]{1,0:T(8,128)S(1)}, f32[512,512]{1,0:T(8,128)S(1)}, bf16[8,128,128]{2,1,0:T(8,128)(2,1)S(1)}) custom-call(bf16[8,128,128]{2,1,0:T(8,128)(2,1)S(1)} %attend.1.att_ref, bf16[256,512]{1,0:T(8,128)(2,1)S(1)} %get-tuple-element.21.own_ref, bf16[256,512]{1,0:T(8,128)(2,1)S(1)} %get-tuple-element.22.upd_ref, ...), custom_call_target="tpu_custom_call" | custom-call | tf_op jit(solution)/shard_map/middle/pallas_call | solution.py:655
  61.9 12.3 %attend_back.1.g_ref = bf16[8,3,128,128]{3,2,1,0:T(8,128)(2,1)S(1)} custom-call(s32[1,4]{1,0:T(1,128)S(1)} %copy-done.5, bf16[16,128,128]{2,1,0:T(8,128)(2,1)S(1)} %get-tuple-element.19.qk_ref, bf16[8,128,128]{2,1,0:T(8,128)(2,1)S(1)} %get-tuple-element.20.v_ref, bf16[8,128,128]{2,1,0:T(8,128)(2,1)S(1)} %get-tuple-element.23.ga_ref), custom_call_target="tpu_custom_call" | custom-call | tf_op jit(solution)/shard_map/attend_back/pallas_call | solution.py:675
  74.2 0.0 copy-done.1
  74.2 51.9 %final.1 = (bf16[256,512]{1,0:T(8,128)(2,1)S(1)}, bf16[640,16,128]{2,1,0:T(8,128)(2,1)S(1)}) custom-call(bf16[8,3,128,128]{3,2,1,0:T(8,128)(2,1)S(1)} %attend_back.1.g_ref, bf16[256,512]{1,0:T(8,128)(2,1)S(1)} %get-tuple-element.21.own_ref, bf16[256,512]{1,0:T(8,128)(2,1)S(1)} %get-tuple-element.24.normed_ref, bf16[512,2048]{1,0:T(8,128)(2,1)S(1)} %copy-done.1, ...), custom_call_target="tpu_custom_call" | custom-call | tf_op jit(solution)/shard_map/final/pallas_call | solution.py:696
  126.1 2.6 %spread.1 = (f32[512,2048]{1,0:T(8,128)}, f32[512,512]{1,0:T(8,128)}, bf16[256,512]{1,0:T(8,128)(2,1)}, bf16[256,512]{1,0:T(8,128)(2,1)}) custom-call(bf16[640,16,128]{2,1,0:T(8,128)(2,1)S(1)} %get-tuple-element.27.sum_ref, bf16[256,512]{1,0:T(8,128)(2,1)S(1)} %get-tuple-element.28.layer_ref, bf16[256,512]{1,0:T(8,128)(2,1)S(1)} %get-tuple-element.29.rowgrad_ref), custom_call_target="tpu_custom_call" | custom-call | tf_op jit(solution)/shard_map/spread/pallas_call | solution.py:721
Async XLA Ops:
  0.6 1.6 %copy-start = (bf16[512,2048]{1,0:T(8,128)(2,1)S(1)}, bf16[512,2048]{1,0:T(8,128)(2,1)}, u32[]{:S(2)}) copy-start(bf16[512,2048]{1,0:T(8,128)(2,1)} %w_ref.1) | copy-start | bytes 6291460
  2.2 0.9 copy-start.4
  3.2 0.7 copy-start.6
  3.9 0.7 copy-start.7
  4.5 42.9 %copy-start.2 = (bf16[256,512]{1,0:T(8,128)(2,1)S(1)}, bf16[256,512]{1,0:T(8,128)(2,1)}, u32[]{:S(2)}) copy-start(bf16[256,512]{1,0:T(8,128)(2,1)} %cot_ref.1) | copy-start | bytes 786436
  4.5 42.9 %copy-start.3 = (bf16[512,512]{1,0:T(8,128)(2,1)S(1)}, bf16[512,512]{1,0:T(8,128)(2,1)}, u32[]{:S(2)}) copy-start(bf16[512,512]{1,0:T(8,128)(2,1)} %wo_hbm.1) | copy-start | bytes 1572868
  38.3 35.9 %copy-start.1 = (bf16[512,2048]{1,0:T(8,128)(2,1)S(1)}, bf16[512,2048]{1,0:T(8,128)(2,1)}, u32[]{:S(2)}) copy-start(bf16[512,2048]{1,0:T(8,128)(2,1)} %w_ref.1) | copy-start | bytes 6291460
  38.3 0.8 copy-start.5

commit v3 on v2

--- a/solution.py
+++ b/solution.py
@@ -20,9 +20,9 @@
 WIDTH = 512
 HD = 64
 EVENTS = 2048
-TILES = 640
 UNITS = 5
 ORDERS = ("zxy", "zyx", "xyz", "yzx", "zxy")
+BACK = ("zxy", "zyx", "zyx", "xzy", "yxz")
 
 
 def normalize(values):
@@ -102,8 +102,8 @@
         load.start()
 
     def device(rel):
-        d = lax.rem(me + rel, ndev)
-        return (d // NCTX, lax.rem(d, NCTX))
+        d = (me + rel) & (ndev - 1)
+        return (d >> 3, d & (NCTX - 1))
 
     barrier = pltpu.get_barrier_semaphore()
 
@@ -111,7 +111,7 @@
         pl.semaphore_signal(barrier, inc=1, device_id=device(rel), device_id_type=MESH)
         return carry
 
-    lax.fori_loop(1, ndev, greet, 0)
+    lax.fori_loop(1, ndev, greet, 0, unroll=6)
 
     for load in loads[:3]:
         load.wait()
@@ -144,7 +144,7 @@
         ).start()
         return carry
 
-    lax.fori_loop(1, ndev, send, 0)
+    lax.fori_loop(1, ndev, send, 0, unroll=6)
     recv[0] = out[0]
     all_rows = pltpu.make_async_remote_copy(
         src_ref=out.at[pl.ds(1, ndev - 1)],
@@ -243,41 +243,49 @@
         dst[(15 - c) * HALF : (16 - c) * HALF, :] = block[:, HD:]
 
 
-def forward_kernel(len_ref, qk_ref, v_ref, att_ref, q, kt, v, att):
-    ends = timeline_ends(len_ref)
-    qk = qk_ref[...].reshape(EVENTS, 128)
-    q[...] = qk[:, :HD]
-    kt[...] = jnp.transpose(qk)[HD:, :]
-    in_position_order(v_ref, v)
-
+def list_pairs(ends, table):
+    count = jnp.int32(0)
     for i in range(NB):
-        row = i * BLK + lax.broadcasted_iota(jnp.int32, (BLK, 1), 0)
-        first = start_of(row, ends)
-        q_i = q[i * BLK : (i + 1) * BLK, :]
-
-        def block(j, acc):
-            at = pl.multiple_of(j * BLK, BLK)
-            h = dot(q_i, kt[:, pl.ds(at, BLK)])
-            w = h + h * jnp.tanh(h)
-            t = at + lax.broadcasted_iota(jnp.int32, (BLK, BLK), 1)
-            w = jnp.where((t >= first) & (t <= row), w, 0.0).astype(BF16)
-            return acc + dot(w, v[pl.ds(at, BLK), :])
-
         lowest = start_of(jnp.int32(i * BLK), ends) >> 8
-        att[i * BLK : (i + 1) * BLK, :] = lax.fori_loop(
-            lowest, i + 1, block, jnp.zeros((BLK, HD), F32)
-        ).astype(BF16)
-
-    for c in range(NCTX):
-        att_ref[c] = jnp.concatenate(
-            [att[c * HALF : (c + 1) * HALF, :], att[(15 - c) * HALF : (16 - c) * HALF, :]], axis=1
-        )
+        for j in range(i + 1):
+            table[count] = i * NB + j
+            count = count + jnp.where(j >= lowest, 1, 0).astype(jnp.int32)
+    return count
+
+
+def for_pairs(unroll, table, count, ends, pair_fn):
+    t = lax.broadcasted_iota(jnp.int32, (BLK, BLK), 0)
+    p = lax.broadcasted_iota(jnp.int32, (1, BLK), 1)
+
+    def step(n, carry):
+        for m in range(unroll):
+            at = n * unroll + m
+            live = at < count
+            pair = jnp.where(live, table[jnp.minimum(at, NB * NB - 1)], 0)
+            i, j = pair >> 3, pair & 7
+            first = jnp.where(live, start_of(p + i * BLK, ends) - j * BLK, BLK)
+            allowed = (t >= first) & (t <= p + (i - j) * BLK)
+            pair_fn(
+                pl.ds(pl.multiple_of(i * BLK, BLK), BLK),
+                pl.ds(pl.multiple_of(j * BLK, BLK), BLK),
+                allowed,
+            )
+        return carry
+
+    lax.fori_loop(0, (count + unroll - 1) // unroll, step, 0)
+
+
+def by_owner(blocks, c):
+    return jnp.concatenate(
+        [blocks[c * HALF : (c + 1) * HALF, :], blocks[(15 - c) * HALF : (16 - c) * HALF, :]], axis=1
+    )
 
 
 def backward_kernel(
-    len_ref, qk_ref, v_ref, ga_ref, g_ref, q, qt, k, kt, v, ga, gat, gqt, gk, gv
+    len_ref, qk_ref, v_ref, ga_ref, g_ref, q, qt, k, kt, v, ga, gat, gqt, gk, gv, table
 ):
     ends = timeline_ends(len_ref)
+    count = list_pairs(ends, table)
     qk = qk_ref[...].reshape(EVENTS, 128)
     q[...] = qk[:, :HD]
     k[...] = qk[:, HD:]
@@ -288,40 +296,27 @@
     in_position_order(ga_ref, ga)
     gat[...] = jnp.transpose(ga[...])
     gqt[...] = jnp.zeros_like(gqt)
-
-    for j in range(NB):
-        t = j * BLK + lax.broadcasted_iota(jnp.int32, (BLK, 1), 0)
-        keys = slice(j * BLK, (j + 1) * BLK)
-        k_j, kt_j, v_j = k[keys, :], kt[:, keys], v[keys, :]
-
-        def block(i, carry):
-            gk_j, gv_j = carry
-            at = pl.multiple_of(i * BLK, BLK)
-            rows = pl.ds(at, BLK)
-            h = dot(k_j, qt[:, rows])
-            u = 1.0 + jnp.tanh(h)
-            w = h * u
-            e = dot(v_j, gat[:, rows]) * (u + w * (2.0 - u))
-            p = at + lax.broadcasted_iota(jnp.int32, (1, BLK), 1)
-            ok = (t >= start_of(p, ends)) & (t <= p)
-            w = jnp.where(ok, w, 0.0).astype(BF16)
-            e = jnp.where(ok, e, 0.0).astype(BF16)
-            gqt[:, rows] += dot(kt_j, e)
-            return gk_j + dot(e, q[rows, :]), gv_j + dot(w, ga[rows, :])
-
-        zero = jnp.zeros((BLK, HD), F32)
-        highest = (end_of(jnp.int32(j * BLK + BLK - 1), ends) - 1) >> 8
-        gk_j, gv_j = lax.fori_loop(j, highest + 1, block, (zero, zero))
-        gk[keys, :] = gk_j.astype(BF16)
-        gv[keys, :] = gv_j.astype(BF16)
-
+    gk[...] = jnp.zeros_like(gk)
+    gv[...] = jnp.zeros_like(gv)
+
+    def pair(rows, keys, allowed):
+        h = dot(k[keys, :], qt[:, rows])
+        u = 1.0 + jnp.tanh(h)
+        w = h * u
+        e = dot(v[keys, :], gat[:, rows]) * (u + w * (2.0 - u))
+        w = jnp.where(allowed, w, 0.0).astype(BF16)
+        e = jnp.where(allowed, e, 0.0).astype(BF16)
+        gqt[:, rows] += dot(kt[:, keys], e)
+        gk[keys, :] += dot(e, q[rows, :])
+        gv[keys, :] += dot(w, ga[rows, :])
+
+    for_pairs(3, table, count, ends, pair)
     gq = jnp.transpose(gqt[...] * 0.0625).astype(BF16)
+    gk_done, gv_done = gk[...].astype(BF16), gv[...].astype(BF16)
     for c in range(NCTX):
-        a = slice(c * HALF, (c + 1) * HALF)
-        b = slice((15 - c) * HALF, (16 - c) * HALF)
-        g_ref[c, 0] = jnp.concatenate([gv[a, :], gv[b, :]], axis=1)
-        g_ref[c, 1] = jnp.concatenate([gq[a, :], gq[b, :]], axis=1)
-        g_ref[c, 2] = jnp.concatenate([gk[a, :], gk[b, :]], axis=1)
+        g_ref[c, 0] = by_owner(gv_done, c)
+        g_ref[c, 1] = by_owner(gq, c)
+        g_ref[c, 2] = by_owner(gk_done, c)
 
 
 def exchange(src, dst, sems, base=0):
@@ -353,11 +348,12 @@
     )
 
 
-def middle_kernel(
-    att_ref, own_ref, upd_ref, cot_hbm, wo_hbm,
+def forward_kernel(
+    len_ref, qk_ref, v_ref, own_ref, upd_ref, cot_hbm, wo_hbm,
     layer_ref, gu_ref, outterm_ref, ga_ref,
-    cot_ref, wo_ref, att_in, ga_msg, sems, in_sems,
+    qt, k, v, vt, att, att_msg, cot_ref, wo_ref, att_in, ga_msg, sems, in_sems,
 ):
+    dp, cx = lax.axis_index("dp"), lax.axis_index("ctx")
     loads = [
         pltpu.make_async_copy(cot_hbm, cot_ref, in_sems.at[0]),
         pltpu.make_async_copy(wo_hbm, wo_ref, in_sems.at[1]),
@@ -365,16 +361,80 @@
     for load in loads:
         load.start()
     barrier = greet_ctx()
+    ends = timeline_ends(len_ref)
+    qk = qk_ref[...].reshape(EVENTS, 128)
+    k[...] = qk[:, HD:]
+    qt[...] = jnp.transpose(qk)[:HD, :]
+    in_position_order(v_ref, v)
+    vt[...] = jnp.transpose(v[...])
+    t = lax.broadcasted_iota(jnp.int32, (BLK, BLK), 0)
+    p = lax.broadcasted_iota(jnp.int32, (1, BLK), 1)
+
+    def to_owner(c):
+        far = pltpu.make_async_remote_copy(
+            src_ref=att_msg.at[c],
+            dst_ref=att_in.at[cx],
+            send_sem=sems.at[c],
+            recv_sem=sems.at[NCTX + cx],
+            device_id=(dp, c),
+            device_id_type=MESH,
+        )
+        return far, pltpu.make_async_copy(att_msg.at[c], att_in.at[cx], sems.at[c])
+
     pl.semaphore_wait(barrier, NCTX - 1)
-    copies = exchange(att_ref, att_in, sems)
+
+    def step(n, carry):
+        block = (n + (cx >> 1)) & 3
+        att[...] = jnp.zeros_like(att)
+        for m in range(9):
+            second = m > block
+            i = jnp.where(second, 7 - block, block)
+            j = jnp.where(second, m - block - 1, m)
+            rows = pl.ds(pl.multiple_of(i * BLK, BLK), BLK)
+            keys = pl.ds(pl.multiple_of(j * BLK, BLK), BLK)
+            h = dot(k[keys, :], qt[:, rows])
+            w = h + h * jnp.tanh(h)
+            first = start_of(p + i * BLK, ends) - j * BLK
+            w = jnp.where((t >= first) & (t <= p + (i - j) * BLK), w, 0.0).astype(BF16)
+            att[jnp.where(second, 1, 0)] += dot(vt[:, keys], w)
+        near_rows = jnp.transpose(att[0]).astype(BF16)
+        far_rows = jnp.transpose(att[1]).astype(BF16)
+        for e in range(2):
+            c = 2 * block + e
+            att_msg[c] = jnp.concatenate(
+                [near_rows[e * HALF : e * HALF + HALF], far_rows[HALF - e * HALF : BLK - e * HALF]], axis=1
+            )
+            far, near = to_owner(c)
+
+            @pl.when(c != cx)
+            def _():
+                far.start()
+
+            @pl.when(c == cx)
+            def _():
+                near.start()
+
+        return carry
+
+    lax.fori_loop(0, 4, step, 0)
     for load in loads:
         load.wait()
     cot = cot_ref[...]
     wo = wo_ref[...]
     grad_gated = dot_nt(cot, wo)
+    to_owner(cx)[1].wait()
+    for rel in range(1, NCTX):
+        h = (cx + rel) & (NCTX - 1)
+        to_owner(h)[0].wait_send()
+        pltpu.make_async_remote_copy(
+            src_ref=att_msg.at[h],
+            dst_ref=att_in.at[h],
+            send_sem=sems.at[h],
+            recv_sem=sems.at[NCTX + h],
+            device_id=(dp, h),
+            device_id_type=MESH,
+        ).wait_recv()
     update = upd_ref[...].astype(F32)
-    for copy in copies:
-        copy.wait()
     attended = gather_heads([att_in[h].astype(F32) for h in range(NCTX)])
     att_normed, inverse = normalize(attended)
     grad_att = normalize_back(grad_gated * update, att_normed, inverse).astype(BF16)
@@ -415,11 +475,6 @@
     for device in [sibling] + [along(axis, r)[1] for axis in "xyz" for r in (1, 2, 3)]:
         pl.semaphore_signal(barrier, inc=1, device_id=device, device_id_type=MESH)
 
-    own, cot = own_ref[...].astype(F32), cot_ref[...]
-    normed, inverse = normalize(own)
-    normed_bf = normed_ref[...]
-    normed_t = jnp.transpose(normed_bf)
-
     def put(u, term):
         for n in range(4):
             part = term[:, n * 128 : n * 128 + 128].reshape(32, 16, 128)
@@ -489,88 +544,122 @@
         for r in range(3):
             total = total + landing[step][r, pl.ds(u * size, size)].astype(F32)
         if step == 2:
-            sum_ref[pl.ds(core * (UNITS * 64) + base[u], size)] = total.astype(BF16)
+            held[u] = [place[axis] for axis in ORDERS[u]]
+            sum_ref[(core, u, *held[u])] = total.astype(BF16)[0]
         else:
             acc[core, pl.ds(base[u], size)] = total
             lead[step + 1][pl.ds(u * size, size)] = total.astype(BF16)
 
+    held = {}
+
     def back_start(u, step):
-        size = sizes[step]
-        held = sum_ref.at[pl.ds(core * (UNITS * 64) + base[u], size)]
-        axis = ORDERS[u][step]
+        axis = BACK[u][step]
+        part = sum_ref.at[(core, u, *held[u])]
         running[u] = [
             remote(
-                held, held, axis_sems.at[2, step, u, r], axis_sems.at[3, step, u, r], along(axis, r)[1]
+                part, part, axis_sems.at[2, step, u, r], axis_sems.at[3, step, u, r], along(axis, r)[1]
             )
             for r in (1, 2, 3)
         ]
-        base[u] = base[u] - place[axis] * size
+        held[u][ORDERS[u].index(axis)] = slice(None)
 
     def core_back(u):
-        held = sum_ref.at[pl.ds((core * UNITS + u) * 64, 64)]
-        running[u] = [remote(held, held, core_sems.at[2, u], core_sems.at[3, u], sibling)]
-
+        part = sum_ref.at[core, u]
+        running[u] = [remote(part, part, core_sems.at[2, u], core_sems.at[3, u], sibling)]
+
+    def after_core(u):
+        core_finish(u)
+        axis_start(u, 0)
+
+    def after_axis(u, step):
+        axis_finish(u, step)
+        if step < 2:
+            axis_start(u, step + 1)
+        else:
+            back_start(u, 0)
+
+    def after_back(u, step):
+        finish(u)
+        if step < 2:
+            back_start(u, step + 1)
+        else:
+            core_back(u)
+
+    pl.semaphore_wait(barrier, NCTX - 1 + 10)
+    g_copies = []
+    for n in range(3):
+        for rel in range(NCTX):
+            peer = (cx + rel) & (NCTX - 1)
+            src, dst = g_ref.at[peer, n], g_in.at[cx, n]
+            if rel == 0:
+                g_copies.append(pltpu.make_async_copy(src, dst, sems.at[n, 0]))
+                g_copies[-1].start()
+            else:
+                g_copies.append(
+                    remote(src, dst, sems.at[n, rel], sems.at[n, NCTX + rel], (dp, peer))
+                )
+
+    own, cot = own_ref[...].astype(F32), cot_ref[...]
+    normed, inverse = normalize(own)
+    normed_bf = normed_ref[...]
+    normed_t = jnp.transpose(normed_bf)
     put(1, outterm_ref[...])
+    core_start(1)
     grad_normed = unit_grads(0, 0, gu_ref[...], silu_grad(dot(normed_bf, columns(0))))
-    pl.semaphore_wait(barrier, NCTX - 1 + 10)
-    g_copies = exchange(g_ref, g_in, sems)
-    early, late = (0, 1), (2, 3, 4)
-    for u in early:
-        core_start(u)
+    core_start(0)
     for n in range(3):
         slope[n] = silu_grad(dot(normed_bf, columns(n + 1)))
-    for u in early:
-        core_finish(u)
-        axis_start(u, 0)
-    for copy in g_copies:
-        copy.wait()
-    for n, u in enumerate(late):
+
+    def late(n, total):
+        for copy in g_copies[n * NCTX : (n + 1) * NCTX]:
+            copy.wait()
         grad = gather_heads([g_in[h, n].astype(F32) for h in range(NCTX)])
-        grad_normed = grad_normed + unit_grads(u, n + 1, grad, slope[n])
-        core_start(u)
+        total = total + unit_grads(n + 2, n + 1, grad, slope[n])
+        core_start(n + 2)
+        return total
+
+    grad_normed = late(0, grad_normed)
+    grad_normed = late(1, grad_normed)
+    after_core(1)
+    after_core(0)
+    grad_normed = late(2, grad_normed)
+    after_core(2)
+    after_core(3)
     rowgrad_ref[...] = (
         cot.astype(F32) + normalize_back(grad_normed, normed, inverse)
     ).astype(BF16)
-    for u in early:
-        axis_finish(u, 0)
-        axis_start(u, 1)
-    for u in late:
-        core_finish(u)
-        axis_start(u, 0)
-    for u in early:
-        axis_finish(u, 1)
-        axis_start(u, 2)
-    for u in late:
-        axis_finish(u, 0)
-        axis_start(u, 1)
-    for u in early:
-        axis_finish(u, 2)
-        back_start(u, 2)
-    for u in late:
-        axis_finish(u, 1)
-        axis_start(u, 2)
-    for u in early:
-        finish(u)
-        back_start(u, 1)
-    for u in late:
-        axis_finish(u, 2)
-        back_start(u, 2)
-    for u in early:
-        finish(u)
-        back_start(u, 0)
-    for u in late:
-        finish(u)
-        back_start(u, 1)
-    for u in early:
-        finish(u)
-        core_back(u)
-    for u in late:
-        finish(u)
-        back_start(u, 0)
-    for u in late:
-        finish(u)
-        core_back(u)
-    for u in early + late:
+    after_core(4)
+    after_axis(1, 0)
+    after_axis(0, 0)
+    after_axis(2, 0)
+    after_axis(3, 0)
+    after_axis(4, 0)
+    after_axis(1, 1)
+    after_axis(0, 1)
+    after_axis(2, 1)
+    after_axis(3, 1)
+    after_axis(4, 1)
+    after_axis(1, 2)
+    after_axis(0, 2)
+    after_axis(2, 2)
+    after_axis(3, 2)
+    after_axis(4, 2)
+    after_back(1, 0)
+    after_back(0, 0)
+    after_back(2, 0)
+    after_back(3, 0)
+    after_back(4, 0)
+    after_back(1, 1)
+    after_back(0, 1)
+    after_back(2, 1)
+    after_back(3, 1)
+    after_back(4, 1)
+    after_back(1, 2)
+    after_back(0, 2)
+    after_back(2, 2)
+    after_back(3, 2)
+    after_back(4, 2)
+    for u in range(UNITS):
         finish(u)
 
 
@@ -583,9 +672,9 @@
         copy.start()
     for u in range(UNITS):
         for n in range(4):
-            at = (n // 2) * UNITS * 64 + u * 64 + (n % 2) * 32
+            at = (n % 2) * 2
             wide[u, :, n * 128 : n * 128 + 128] = (
-                sum_ref[at : at + 32].reshape(WIDTH, 128).astype(F32) * scale
+                sum_ref[n // 2, u, at : at + 2].reshape(WIDTH, 128).astype(F32) * scale
             )
         block = (0, None, 1, 2, 3)[u]
         dst = out_hbm if block is None else proj_hbm.at[:, pl.ds(block * WIDTH, WIDTH)]
@@ -604,8 +693,12 @@
     return jax.ShapeDtypeStruct(dims, dtype)
 
 
-def params(**kw):
-    return pltpu.CompilerParams(vmem_limit_bytes=VMEM_LIMIT, **kw)
+def params(vmem_limit_bytes=VMEM_LIMIT, **kw):
+    return pltpu.CompilerParams(vmem_limit_bytes=vmem_limit_bytes, **kw)
+
+
+def in_hbm(array):
+    return pltpu.with_memory_space_constraint(array, pltpu.HBM)
 
 
 def local(loader_rows, send_slot, arrive_slot, user_lengths, proj_weight, out_weight, cotangent):
@@ -635,33 +728,26 @@
             pltpu.SemaphoreType.DMA((4,)),
         ],
         compiler_params=params(collective_id=0, has_side_effects=True),
-    )(loader_rows, send_slot.reshape(1, BLK), arrive_slot.reshape(1, BLK), proj_weight)
-
-    att = pl.pallas_call(
+    )(
+        *map(in_hbm, (loader_rows, send_slot.reshape(1, BLK), arrive_slot.reshape(1, BLK), proj_weight))
+    )
+
+    layer_out, grad_update, out_term, grad_att = pl.pallas_call(
         forward_kernel,
-        name="attend",
-        out_shape=shape(NCTX, HALF, 128),
-        in_specs=[SM, VM, VM],
-        out_specs=VM,
-        scratch_shapes=[
-            pltpu.VMEM((EVENTS, HD), BF16),
-            pltpu.VMEM((HD, EVENTS), BF16),
-            pltpu.VMEM((EVENTS, HD), BF16),
-            pltpu.VMEM((EVENTS, HD), BF16),
-        ],
-        compiler_params=params(),
-    )(user_lengths, qk, v)
-
-    layer_out, grad_update, out_term, grad_att = pl.pallas_call(
-        middle_kernel,
-        name="middle",
+        name="forward",
         out_shape=(
             shape(BLK, WIDTH), shape(BLK, WIDTH, dtype=F32), shape(WIDTH, WIDTH, dtype=F32),
             shape(NCTX, HALF, 128),
         ),
-        in_specs=[VM, VM, VM, HBM, HBM],
+        in_specs=[SM, VM, VM, VM, VM, HBM, HBM],
         out_specs=(VM,) * 4,
         scratch_shapes=[
+            pltpu.VMEM((HD, EVENTS), BF16),
+            pltpu.VMEM((EVENTS, HD), BF16),
+            pltpu.VMEM((EVENTS, HD), BF16),
+            pltpu.VMEM((HD, EVENTS), BF16),
+            pltpu.VMEM((2, HD, BLK), F32),
+            pltpu.VMEM((NCTX, HALF, 128), BF16),
             pltpu.VMEM((BLK, WIDTH), BF16),
             pltpu.VMEM((WIDTH, WIDTH), BF16),
             pltpu.VMEM((NCTX, HALF, 128), BF16),
@@ -670,7 +756,7 @@
             pltpu.SemaphoreType.DMA((2,)),
         ],
         compiler_params=params(collective_id=1, has_side_effects=True),
-    )(att, own, update, cotangent, out_weight)
+    )(in_hbm(user_lengths), qk, v, own, update, in_hbm(cotangent), in_hbm(out_weight))
 
     grads = pl.pallas_call(
         backward_kernel,
@@ -687,16 +773,17 @@
             pltpu.VMEM((EVENTS, HD), BF16),
             pltpu.VMEM((HD, EVENTS), BF16),
             pltpu.VMEM((HD, EVENTS), F32),
-            pltpu.VMEM((EVENTS, HD), BF16),
-            pltpu.VMEM((EVENTS, HD), BF16),
+            pltpu.VMEM((EVENTS, HD), F32),
+            pltpu.VMEM((EVENTS, HD), F32),
+            pltpu.SMEM((NB * NB,), jnp.int32),
         ],
         compiler_params=params(),
-    )(user_lengths, qk, v, grad_att)
+    )(in_hbm(user_lengths), qk, v, grad_att)
 
     row_grads, sums = pl.pallas_call(
         final_kernel,
         name="final",
-        out_shape=(shape(BLK, WIDTH), shape(TILES, 16, 128)),
+        out_shape=(shape(BLK, WIDTH), shape(2, UNITS, 4, 4, 4, 16, 128)),
         in_specs=[VM] * 7,
         out_specs=(VM,) * 2,
         scratch_shapes=[
@@ -711,7 +798,7 @@
             pltpu.VMEM((3, UNITS * 4, 16, 128), BF16),
             pltpu.VMEM((UNITS * 4, 16, 128), BF16),
             pltpu.VMEM((3, UNITS, 16, 128), BF16),
-            pltpu.SemaphoreType.DMA((2 * NCTX,)),
+            pltpu.SemaphoreType.DMA((3, 2 * NCTX)),
             pltpu.SemaphoreType.DMA((4, UNITS)),
             pltpu.SemaphoreType.DMA((4, 3, UNITS, 4)),
         ],

time: 129 us -> 119 us (0.922)
  Pallas kernels: 123 us -> 118 us
  local copies, waits for them, and re-layouts: 4.7 us -> 0.01 us
    unnamed x16 -> x4, local copies, waits for them, and re-layouts: 4.7 us -> 0.01 us
    pallas_call x1, Pallas kernels: 51.9 us -> 47.6 us  [local(): pl.pallas_call(final_kernel, name='final', out_shape=(shape(BLK, WIDTH),...]
    pallas_call x2 -> x1, Pallas kernels: 22.8 us -> 22.3 us  [local(): pl.pallas_call(forward_kernel, name='forward', out_shape=(shape(BLK, WIDT...]
where the time goes in v3:
time: 119 us; the launch traced here: 118 us
  Pallas kernels  118 us (99%)
    pallas_call x1, Pallas kernels, local(): pl.pallas_call(final_kernel, name='final', out_shape=(shape(BLK, WIDTH),...  47.6 us
    pallas_call x1, Pallas kernels, local(): pl.pallas_call(arrive_kernel, name='arrive', out_shape=(shape(BLK, WIDTH)...  33 us
    pallas_call x1, Pallas kernels, local(): pl.pallas_call(forward_kernel, name='forward', out_shape=(shape(BLK, WIDT...  22.3 us
    pallas_call x1, Pallas kernels, local(): pl.pallas_call(backward_kernel, name='attend_back', out_shape=shape(NCTX,...  12.2 us
    pallas_call x1, Pallas kernels, local(): pl.pallas_call(functools.partial(spread_kernel, (BLK * 128) ** (-0.5)), n...  2.59 us

profile of v3, /device:TPU:1, one launch (start us, length us, event | category | flops | bytes accessed | tf_op | source)
XLA Modules:
  0.0 118.5 jit_solution(3499899740725820692)
XLA Ops:
  0.6 0.0 copy-start
  0.6 0.0 copy-start.1
  0.7 33.0 %arrive.1 = (bf16[256,512]{1,0:T(8,128)(2,1)S(1)}, bf16[256,512]{1,0:T(8,128)(2,1)S(1)}, bf16[256,512]{1,0:T(8,128)(2,1)S(1)}, bf16[16,128,128]{2,1,0:T(8,128)(2,1)S(1)}, bf16[8,128,128]{2,1,0:T(8,128)(2,1)S(1)}) custom-call(bf16[256,512]{1,0:T(8,128)(2,1)} %rows_hbm.1, s32[1,256]{1,0:T(1,128)} %bitcast.2, s32[1,256]{1,0:T(1,128)} %bitcast.3, ...), custom_call_target="tpu_custom_call" | custom-call | tf_op jit(solution)/shard_map/arrive/pallas_call | solution.py:705
  33.6 22.3 %forward.1 = (bf16[256,512]{1,0:T(8,128)(2,1)S(1)}, f32[256,512]{1,0:T(8,128)S(1)}, f32[512,512]{1,0:T(8,128)S(1)}, bf16[8,128,128]{2,1,0:T(8,128)(2,1)S(1)}) custom-call(s32[1,4]{1,0:T(1,128)} %len_ref.3, bf16[16,128,128]{2,1,0:T(8,128)(2,1)S(1)} %get-tuple-element.19.qk_ref, bf16[8,128,128]{2,1,0:T(8,128)(2,1)S(1)} %get-tuple-element.20.v_ref, ...), custom_call_target="tpu_custom_call" | custom-call | tf_op jit(solution)/shard_map/forward/pallas_call | solution.py:735
  55.9 12.2 %attend_back.1.g_ref = bf16[8,3,128,128]{3,2,1,0:T(8,128)(2,1)S(1)} custom-call(s32[1,4]{1,0:T(1,128)} %len_ref.3, bf16[16,128,128]{2,1,0:T(8,128)(2,1)S(1)} %get-tuple-element.19.qk_ref, bf16[8,128,128]{2,1,0:T(8,128)(2,1)S(1)} %get-tuple-element.20.v_ref, bf16[8,128,128]{2,1,0:T(8,128)(2,1)S(1)} %get-tuple-element.23.ga_ref), custom_call_target="tpu_custom_call" | custom-call | tf_op jit(solution)/shard_map/attend_back/pallas_call | solution.py:761
  68.1 0.0 copy-done
  68.1 0.0 copy-done.1
  68.1 47.6 %final.1 = (bf16[256,512]{1,0:T(8,128)(2,1)S(1)}, bf16[2,5,4,4,4,16,128]{6,5,4,3,2,1,0:T(8,128)(2,1)S(1)}) custom-call(bf16[8,3,128,128]{3,2,1,0:T(8,128)(2,1)S(1)} %attend_back.1.g_ref, bf16[256,512]{1,0:T(8,128)(2,1)S(1)} %get-tuple-element.21.own_ref, bf16[256,512]{1,0:T(8,128)(2,1)S(1)} %get-tuple-element.24.normed_ref, bf16[512,2048]{1,0:T(8,128)(2,1)S(1)} %copy-done, ...), custom_call_target="tpu_custom_call" | custom-call | tf_op jit(solution)/shard_map/final/pallas_call | solution.py:783
  115.7 2.6 %spread.1 = (f32[512,2048]{1,0:T(8,128)}, f32[512,512]{1,0:T(8,128)}, bf16[256,512]{1,0:T(8,128)(2,1)}, bf16[256,512]{1,0:T(8,128)(2,1)}) custom-call(bf16[2,5,4,4,4,16,128]{6,5,4,3,2,1,0:T(8,128)(2,1)S(1)} %get-tuple-element.27.sum_ref, bf16[256,512]{1,0:T(8,128)(2,1)S(1)} %get-tuple-element.28.layer_ref, bf16[256,512]{1,0:T(8,128)(2,1)S(1)} %get-tuple-element.29.rowgrad_ref), custom_call_target="tpu_custom_call" | custom-call | tf_op jit(solution)/shard_map/spread/pallas_call | solution.py:808
Async XLA Ops:
  0.6 67.4 %copy-start = (bf16[512,2048]{1,0:T(8,128)(2,1)S(1)}, bf16[512,2048]{1,0:T(8,128)(2,1)}, u32[]{:S(2)}) copy-start(bf16[512,2048]{1,0:T(8,128)(2,1)} %w_ref.1) | copy-start | bytes 6291460
  0.6 67.4 %copy-start.1 = (bf16[256,512]{1,0:T(8,128)(2,1)S(1)}, bf16[256,512]{1,0:T(8,128)(2,1)}, u32[]{:S(2)}) copy-start(bf16[256,512]{1,0:T(8,128)(2,1)} %cot_ref.1) | copy-start | bytes 786436

commit v4 on v3

--- a/solution.py
+++ b/solution.py
@@ -243,38 +243,6 @@
         dst[(15 - c) * HALF : (16 - c) * HALF, :] = block[:, HD:]
 
 
-def list_pairs(ends, table):
-    count = jnp.int32(0)
-    for i in range(NB):
-        lowest = start_of(jnp.int32(i * BLK), ends) >> 8
-        for j in range(i + 1):
-            table[count] = i * NB + j
-            count = count + jnp.where(j >= lowest, 1, 0).astype(jnp.int32)
-    return count
-
-
-def for_pairs(unroll, table, count, ends, pair_fn):
-    t = lax.broadcasted_iota(jnp.int32, (BLK, BLK), 0)
-    p = lax.broadcasted_iota(jnp.int32, (1, BLK), 1)
-
-    def step(n, carry):
-        for m in range(unroll):
-            at = n * unroll + m
-            live = at < count
-            pair = jnp.where(live, table[jnp.minimum(at, NB * NB - 1)], 0)
-            i, j = pair >> 3, pair & 7
-            first = jnp.where(live, start_of(p + i * BLK, ends) - j * BLK, BLK)
-            allowed = (t >= first) & (t <= p + (i - j) * BLK)
-            pair_fn(
-                pl.ds(pl.multiple_of(i * BLK, BLK), BLK),
-                pl.ds(pl.multiple_of(j * BLK, BLK), BLK),
-                allowed,
-            )
-        return carry
-
-    lax.fori_loop(0, (count + unroll - 1) // unroll, step, 0)
-
-
 def by_owner(blocks, c):
     return jnp.concatenate(
         [blocks[c * HALF : (c + 1) * HALF, :], blocks[(15 - c) * HALF : (16 - c) * HALF, :]], axis=1
@@ -282,10 +250,9 @@
 
 
 def backward_kernel(
-    len_ref, qk_ref, v_ref, ga_ref, g_ref, q, qt, k, kt, v, ga, gat, gqt, gk, gv, table
+    len_ref, qk_ref, v_ref, ga_ref, g_ref, q, qt, k, kt, v, ga, gat, gqt, gk, gv
 ):
     ends = timeline_ends(len_ref)
-    count = list_pairs(ends, table)
     qk = qk_ref[...].reshape(EVENTS, 128)
     q[...] = qk[:, :HD]
     k[...] = qk[:, HD:]
@@ -299,18 +266,39 @@
     gk[...] = jnp.zeros_like(gk)
     gv[...] = jnp.zeros_like(gv)
 
-    def pair(rows, keys, allowed):
-        h = dot(k[keys, :], qt[:, rows])
-        u = 1.0 + jnp.tanh(h)
-        w = h * u
-        e = dot(v[keys, :], gat[:, rows]) * (u + w * (2.0 - u))
-        w = jnp.where(allowed, w, 0.0).astype(BF16)
-        e = jnp.where(allowed, e, 0.0).astype(BF16)
-        gqt[:, rows] += dot(kt[:, keys], e)
-        gk[keys, :] += dot(e, q[rows, :])
-        gv[keys, :] += dot(w, ga[rows, :])
-
-    for_pairs(3, table, count, ends, pair)
+    t = lax.broadcasted_iota(jnp.int32, (BLK, BLK), 0)
+    p = lax.broadcasted_iota(jnp.int32, (1, BLK), 1)
+
+    def blocks(i, keys_of):
+        rows = slice(i * BLK, (i + 1) * BLK)
+        first = start_of(p + i * BLK, ends)
+        query, parts = 0.0, []
+        for j in keys_of:
+            keys = slice(j * BLK, (j + 1) * BLK)
+            allowed = t >= first - j * BLK
+            if j == i:
+                allowed = allowed & (t <= p)
+            h = dot(k[keys, :], qt[:, rows])
+            u = 1.0 + jnp.tanh(h)
+            w = h * u
+            e = dot(v[keys, :], gat[:, rows]) * (u + w * (2.0 - u))
+            w = jnp.where(allowed, w, 0.0).astype(BF16)
+            e = jnp.where(allowed, e, 0.0).astype(BF16)
+            query = query + dot(kt[:, keys], e)
+            parts.append((keys, dot(e, q[rows, :]), dot(w, ga[rows, :])))
+        gqt[:, rows] += query
+        for keys, key, value in parts:
+            gk[keys, :] += key
+            gv[keys, :] += value
+
+    for i in range(NB):
+        lowest = start_of(jnp.int32(i * BLK), ends) >> 8
+        blocks(i, range(i, max(i - 3, -1), -1))
+        for top in range(i - 3, -1, -3):
+            pl.when(lowest <= top)(
+                functools.partial(blocks, i, range(top, max(top - 3, -1), -1))
+            )
+
     gq = jnp.transpose(gqt[...] * 0.0625).astype(BF16)
     gk_done, gv_done = gk[...].astype(BF16), gv[...].astype(BF16)
     for c in range(NCTX):
@@ -351,7 +339,7 @@
 def forward_kernel(
     len_ref, qk_ref, v_ref, own_ref, upd_ref, cot_hbm, wo_hbm,
     layer_ref, gu_ref, outterm_ref, ga_ref,
-    qt, k, v, vt, att, att_msg, cot_ref, wo_ref, att_in, ga_msg, sems, in_sems,
+    qt, k, v, vt, att_msg, cot_ref, wo_ref, att_in, ga_msg, sems, in_sems,
 ):
     dp, cx = lax.axis_index("dp"), lax.axis_index("ctx")
     loads = [
@@ -385,7 +373,8 @@
 
     def step(n, carry):
         block = (n + (cx >> 1)) & 3
-        att[...] = jnp.zeros_like(att)
+        near_sum = jnp.zeros((HD, BLK), F32)
+        far_sum = jnp.zeros((HD, BLK), F32)
         for m in range(9):
             second = m > block
             i = jnp.where(second, 7 - block, block)
@@ -396,9 +385,16 @@
             w = h + h * jnp.tanh(h)
             first = start_of(p + i * BLK, ends) - j * BLK
             w = jnp.where((t >= first) & (t <= p + (i - j) * BLK), w, 0.0).astype(BF16)
-            att[jnp.where(second, 1, 0)] += dot(vt[:, keys], w)
-        near_rows = jnp.transpose(att[0]).astype(BF16)
-        far_rows = jnp.transpose(att[1]).astype(BF16)
+            part = dot(vt[:, keys], w)
+            if m == 0:
+                near_sum = part
+            elif m > 3:
+                far_sum = far_sum + part
+            else:
+                near_sum = near_sum + jnp.where(second, 0.0, part)
+                far_sum = far_sum + jnp.where(second, part, 0.0)
+        near_rows = jnp.transpose(near_sum).astype(BF16)
+        far_rows = jnp.transpose(far_sum).astype(BF16)
         for e in range(2):
             c = 2 * block + e
             att_msg[c] = jnp.concatenate(
@@ -746,7 +742,6 @@
             pltpu.VMEM((EVENTS, HD), BF16),
             pltpu.VMEM((EVENTS, HD), BF16),
             pltpu.VMEM((HD, EVENTS), BF16),
-            pltpu.VMEM((2, HD, BLK), F32),
             pltpu.VMEM((NCTX, HALF, 128), BF16),
             pltpu.VMEM((BLK, WIDTH), BF16),
             pltpu.VMEM((WIDTH, WIDTH), BF16),
@@ -775,7 +770,6 @@
             pltpu.VMEM((HD, EVENTS), F32),
             pltpu.VMEM((EVENTS, HD), F32),
             pltpu.VMEM((EVENTS, HD), F32),
-            pltpu.SMEM((NB * NB,), jnp.int32),
         ],
         compiler_params=params(),
     )(in_hbm(user_lengths), qk, v, grad_att)

time: 119 us -> 116 us (0.975)
  Pallas kernels: 118 us -> 115 us
    pallas_call x1, Pallas kernels: 22.3 us -> 20.7 us  [local(): pl.pallas_call(forward_kernel, name='forward', out_shape=(shape(BLK, WIDT...]
    pallas_call x1, Pallas kernels: 12.2 us -> 10.8 us  [local(): pl.pallas_call(backward_kernel, name='attend_back', out_shape=shape(NCTX,...]
where the time goes in v4:
time: 116 us
  Pallas kernels  115 us (99%)
    pallas_call x1, Pallas kernels, local(): pl.pallas_call(final_kernel, name='final', out_shape=(shape(BLK, WIDTH),...  48 us
    pallas_call x1, Pallas kernels, local(): pl.pallas_call(arrive_kernel, name='arrive', out_shape=(shape(BLK, WIDTH)...  33 us
    pallas_call x1, Pallas kernels, local(): pl.pallas_call(forward_kernel, name='forward', out_shape=(shape(BLK, WIDT...  20.7 us
    pallas_call x1, Pallas kernels, local(): pl.pallas_call(backward_kernel, name='attend_back', out_shape=shape(NCTX,...  10.8 us
    pallas_call x1, Pallas kernels, local(): pl.pallas_call(functools.partial(spread_kernel, (BLK * 128) ** (-0.5)), n...  2.59 us

profile of v4, /device:TPU:1, one launch (start us, length us, event | category | flops | bytes accessed | tf_op | source)
XLA Modules:
  0.0 116.0 jit_solution(3487073234607855061)
XLA Ops:
  0.6 0.0 copy-start
  0.6 0.0 copy-start.1
  0.7 33.0 %arrive.1 = (bf16[256,512]{1,0:T(8,128)(2,1)S(1)}, bf16[256,512]{1,0:T(8,128)(2,1)S(1)}, bf16[256,512]{1,0:T(8,128)(2,1)S(1)}, bf16[16,128,128]{2,1,0:T(8,128)(2,1)S(1)}, bf16[8,128,128]{2,1,0:T(8,128)(2,1)S(1)}) custom-call(bf16[256,512]{1,0:T(8,128)(2,1)} %rows_hbm.1, s32[1,256]{1,0:T(1,128)} %bitcast.2, s32[1,256]{1,0:T(1,128)} %bitcast.3, ...), custom_call_target="tpu_custom_call" | custom-call | tf_op jit(solution)/shard_map/arrive/pallas_call | solution.py:701
  33.6 20.7 %forward.1 = (bf16[256,512]{1,0:T(8,128)(2,1)S(1)}, f32[256,512]{1,0:T(8,128)S(1)}, f32[512,512]{1,0:T(8,128)S(1)}, bf16[8,128,128]{2,1,0:T(8,128)(2,1)S(1)}) custom-call(s32[1,4]{1,0:T(1,128)} %len_ref.3, bf16[16,128,128]{2,1,0:T(8,128)(2,1)S(1)} %get-tuple-element.19.qk_ref, bf16[8,128,128]{2,1,0:T(8,128)(2,1)S(1)} %get-tuple-element.20.v_ref, ...), custom_call_target="tpu_custom_call" | custom-call | tf_op jit(solution)/shard_map/forward/pallas_call | solution.py:731
  54.3 10.8 %attend_back.1.g_ref = bf16[8,3,128,128]{3,2,1,0:T(8,128)(2,1)S(1)} custom-call(s32[1,4]{1,0:T(1,128)} %len_ref.3, bf16[16,128,128]{2,1,0:T(8,128)(2,1)S(1)} %get-tuple-element.19.qk_ref, bf16[8,128,128]{2,1,0:T(8,128)(2,1)S(1)} %get-tuple-element.20.v_ref, bf16[8,128,128]{2,1,0:T(8,128)(2,1)S(1)} %get-tuple-element.23.ga_ref), custom_call_target="tpu_custom_call" | custom-call | tf_op jit(solution)/shard_map/attend_back/pallas_call | solution.py:756
  65.2 0.0 copy-done
  65.2 0.0 copy-done.1
  65.2 48.0 %final.1 = (bf16[256,512]{1,0:T(8,128)(2,1)S(1)}, bf16[2,5,4,4,4,16,128]{6,5,4,3,2,1,0:T(8,128)(2,1)S(1)}) custom-call(bf16[8,3,128,128]{3,2,1,0:T(8,128)(2,1)S(1)} %attend_back.1.g_ref, bf16[256,512]{1,0:T(8,128)(2,1)S(1)} %get-tuple-element.21.own_ref, bf16[256,512]{1,0:T(8,128)(2,1)S(1)} %get-tuple-element.24.normed_ref, bf16[512,2048]{1,0:T(8,128)(2,1)S(1)} %copy-done, ...), custom_call_target="tpu_custom_call" | custom-call | tf_op jit(solution)/shard_map/final/pallas_call | solution.py:777
  113.2 2.6 %spread.1 = (f32[512,2048]{1,0:T(8,128)}, f32[512,512]{1,0:T(8,128)}, bf16[256,512]{1,0:T(8,128)(2,1)}, bf16[256,512]{1,0:T(8,128)(2,1)}) custom-call(bf16[2,5,4,4,4,16,128]{6,5,4,3,2,1,0:T(8,128)(2,1)S(1)} %get-tuple-element.27.sum_ref, bf16[256,512]{1,0:T(8,128)(2,1)S(1)} %get-tuple-element.28.layer_ref, bf16[256,512]{1,0:T(8,128)(2,1)S(1)} %get-tuple-element.29.rowgrad_ref), custom_call_target="tpu_custom_call" | custom-call | tf_op jit(solution)/shard_map/spread/pallas_call | solution.py:802
Async XLA Ops:
  0.6 64.5 %copy-start = (bf16[512,2048]{1,0:T(8,128)(2,1)S(1)}, bf16[512,2048]{1,0:T(8,128)(2,1)}, u32[]{:S(2)}) copy-start(bf16[512,2048]{1,0:T(8,128)(2,1)} %w_ref.1) | copy-start | bytes 6291460
  0.6 64.5 %copy-start.1 = (bf16[256,512]{1,0:T(8,128)(2,1)S(1)}, bf16[256,512]{1,0:T(8,128)(2,1)}, u32[]{:S(2)}) copy-start(bf16[256,512]{1,0:T(8,128)(2,1)} %cot_ref.1) | copy-start | bytes 786436

commit v5 on v4

--- a/solution.py
+++ b/solution.py
@@ -368,8 +368,6 @@
             device_id_type=MESH,
         )
         return far, pltpu.make_async_copy(att_msg.at[c], att_in.at[cx], sems.at[c])
-
-    pl.semaphore_wait(barrier, NCTX - 1)
 
     def step(n, carry):
         block = (n + (cx >> 1)) & 3
@@ -395,6 +393,11 @@
                 far_sum = far_sum + jnp.where(second, part, 0.0)
         near_rows = jnp.transpose(near_sum).astype(BF16)
         far_rows = jnp.transpose(far_sum).astype(BF16)
+
+        @pl.when(n == 0)
+        def _():
+            pl.semaphore_wait(barrier, NCTX - 1)
+
         for e in range(2):
             c = 2 * block + e
             att_msg[c] = jnp.concatenate(

time: 116 us -> 114 us (0.983)
  Pallas kernels: 115 us -> 113 us
    pallas_call x1, Pallas kernels: 20.7 us -> 19.1 us  [local(): pl.pallas_call(forward_kernel, name='forward', out_shape=(shape(BLK, WIDT...]
where the time goes in v5:
time: 114 us
  Pallas kernels  113 us (99%)
    pallas_call x1, Pallas kernels, local(): pl.pallas_call(final_kernel, name='final', out_shape=(shape(BLK, WIDTH),...  47.3 us
    pallas_call x1, Pallas kernels, local(): pl.pallas_call(arrive_kernel, name='arrive', out_shape=(shape(BLK, WIDTH)...  33 us
    pallas_call x1, Pallas kernels, local(): pl.pallas_call(forward_kernel, name='forward', out_shape=(shape(BLK, WIDT...  19.1 us
    pallas_call x1, Pallas kernels, local(): pl.pallas_call(backward_kernel, name='attend_back', out_shape=shape(NCTX,...  11.4 us
    pallas_call x1, Pallas kernels, local(): pl.pallas_call(functools.partial(spread_kernel, (BLK * 128) ** (-0.5)), n...  2.59 us

profile of v5, /device:TPU:1, one launch (start us, length us, event | category | flops | bytes accessed | tf_op | source)
XLA Modules:
  0.0 114.2 jit_solution(6177590525581747388)
XLA Ops:
  0.6 0.0 copy-start
  0.6 0.0 copy-start.1
  0.7 33.0 %arrive.1 = (bf16[256,512]{1,0:T(8,128)(2,1)S(1)}, bf16[256,512]{1,0:T(8,128)(2,1)S(1)}, bf16[256,512]{1,0:T(8,128)(2,1)S(1)}, bf16[16,128,128]{2,1,0:T(8,128)(2,1)S(1)}, bf16[8,128,128]{2,1,0:T(8,128)(2,1)S(1)}) custom-call(bf16[256,512]{1,0:T(8,128)(2,1)} %rows_hbm.1, s32[1,256]{1,0:T(1,128)} %bitcast.2, s32[1,256]{1,0:T(1,128)} %bitcast.3, ...), custom_call_target="tpu_custom_call" | custom-call | tf_op jit(solution)/shard_map/arrive/pallas_call | solution.py:704
  33.6 19.1 %forward.1 = (bf16[256,512]{1,0:T(8,128)(2,1)S(1)}, f32[256,512]{1,0:T(8,128)S(1)}, f32[512,512]{1,0:T(8,128)S(1)}, bf16[8,128,128]{2,1,0:T(8,128)(2,1)S(1)}) custom-call(s32[1,4]{1,0:T(1,128)} %len_ref.3, bf16[16,128,128]{2,1,0:T(8,128)(2,1)S(1)} %get-tuple-element.19.qk_ref, bf16[8,128,128]{2,1,0:T(8,128)(2,1)S(1)} %get-tuple-element.20.v_ref, ...), custom_call_target="tpu_custom_call" | custom-call | tf_op jit(solution)/shard_map/forward/pallas_call | solution.py:734
  52.8 11.4 %attend_back.1.g_ref = bf16[8,3,128,128]{3,2,1,0:T(8,128)(2,1)S(1)} custom-call(s32[1,4]{1,0:T(1,128)} %len_ref.3, bf16[16,128,128]{2,1,0:T(8,128)(2,1)S(1)} %get-tuple-element.19.qk_ref, bf16[8,128,128]{2,1,0:T(8,128)(2,1)S(1)} %get-tuple-element.20.v_ref, bf16[8,128,128]{2,1,0:T(8,128)(2,1)S(1)} %get-tuple-element.23.ga_ref), custom_call_target="tpu_custom_call" | custom-call | tf_op jit(solution)/shard_map/attend_back/pallas_call | solution.py:759
  64.2 0.0 copy-done
  64.2 0.0 copy-done.1
  64.2 47.3 %final.1 = (bf16[256,512]{1,0:T(8,128)(2,1)S(1)}, bf16[2,5,4,4,4,16,128]{6,5,4,3,2,1,0:T(8,128)(2,1)S(1)}) custom-call(bf16[8,3,128,128]{3,2,1,0:T(8,128)(2,1)S(1)} %attend_back.1.g_ref, bf16[256,512]{1,0:T(8,128)(2,1)S(1)} %get-tuple-element.21.own_ref, bf16[256,512]{1,0:T(8,128)(2,1)S(1)} %get-tuple-element.24.normed_ref, bf16[512,2048]{1,0:T(8,128)(2,1)S(1)} %copy-done, ...), custom_call_target="tpu_custom_call" | custom-call | tf_op jit(solution)/shard_map/final/pallas_call | solution.py:780
  111.5 2.6 %spread.1 = (f32[512,2048]{1,0:T(8,128)}, f32[512,512]{1,0:T(8,128)}, bf16[256,512]{1,0:T(8,128)(2,1)}, bf16[256,512]{1,0:T(8,128)(2,1)}) custom-call(bf16[2,5,4,4,4,16,128]{6,5,4,3,2,1,0:T(8,128)(2,1)S(1)} %get-tuple-element.27.sum_ref, bf16[256,512]{1,0:T(8,128)(2,1)S(1)} %get-tuple-element.28.layer_ref, bf16[256,512]{1,0:T(8,128)(2,1)S(1)} %get-tuple-element.29.rowgrad_ref), custom_call_target="tpu_custom_call" | custom-call | tf_op jit(solution)/shard_map/spread/pallas_call | solution.py:805
Async XLA Ops:
  0.6 63.5 %copy-start = (bf16[512,2048]{1,0:T(8,128)(2,1)S(1)}, bf16[512,2048]{1,0:T(8,128)(2,1)}, u32[]{:S(2)}) copy-start(bf16[512,2048]{1,0:T(8,128)(2,1)} %w_ref.1) | copy-start | bytes 6291460
  0.6 63.5 %copy-start.1 = (bf16[256,512]{1,0:T(8,128)(2,1)S(1)}, bf16[256,512]{1,0:T(8,128)(2,1)}, u32[]{:S(2)}) copy-start(bf16[256,512]{1,0:T(8,128)(2,1)} %cot_ref.1) | copy-start | bytes 786436

commit v6 on v5

--- a/solution.py
+++ b/solution.py
@@ -618,9 +618,9 @@
         return total
 
     grad_normed = late(0, grad_normed)
-    grad_normed = late(1, grad_normed)
     after_core(1)
     after_core(0)
+    grad_normed = late(1, grad_normed)
     grad_normed = late(2, grad_normed)
     after_core(2)
     after_core(3)

time: 114 us -> 113 us (level)
  no operation moved by 1% of the time
where the time goes in v6:
time: 113 us
  Pallas kernels  113 us (100%)
    pallas_call x1, Pallas kernels, local(): pl.pallas_call(final_kernel, name='final', out_shape=(shape(BLK, WIDTH),...  46.4 us
    pallas_call x1, Pallas kernels, local(): pl.pallas_call(arrive_kernel, name='arrive', out_shape=(shape(BLK, WIDTH)...  33 us
    pallas_call x1, Pallas kernels, local(): pl.pallas_call(forward_kernel, name='forward', out_shape=(shape(BLK, WIDT...  19.1 us
    pallas_call x1, Pallas kernels, local(): pl.pallas_call(backward_kernel, name='attend_back', out_shape=shape(NCTX,...  11.4 us
    pallas_call x1, Pallas kernels, local(): pl.pallas_call(functools.partial(spread_kernel, (BLK * 128) ** (-0.5)), n...  2.59 us

profile of v6, /device:TPU:1, one launch (start us, length us, event | category | flops | bytes accessed | tf_op | source)
XLA Modules:
  0.0 113.4 jit_solution(15052815586455327752)
XLA Ops:
  0.6 0.0 copy-start
  0.6 0.0 copy-start.1
  0.7 33.0 %arrive.1 = (bf16[256,512]{1,0:T(8,128)(2,1)S(1)}, bf16[256,512]{1,0:T(8,128)(2,1)S(1)}, bf16[256,512]{1,0:T(8,128)(2,1)S(1)}, bf16[16,128,128]{2,1,0:T(8,128)(2,1)S(1)}, bf16[8,128,128]{2,1,0:T(8,128)(2,1)S(1)}) custom-call(bf16[256,512]{1,0:T(8,128)(2,1)} %rows_hbm.1, s32[1,256]{1,0:T(1,128)} %bitcast.2, s32[1,256]{1,0:T(1,128)} %bitcast.3, ...), custom_call_target="tpu_custom_call" | custom-call | tf_op jit(solution)/shard_map/arrive/pallas_call | solution.py:704
  33.6 19.1 %forward.1 = (bf16[256,512]{1,0:T(8,128)(2,1)S(1)}, f32[256,512]{1,0:T(8,128)S(1)}, f32[512,512]{1,0:T(8,128)S(1)}, bf16[8,128,128]{2,1,0:T(8,128)(2,1)S(1)}) custom-call(s32[1,4]{1,0:T(1,128)} %len_ref.3, bf16[16,128,128]{2,1,0:T(8,128)(2,1)S(1)} %get-tuple-element.19.qk_ref, bf16[8,128,128]{2,1,0:T(8,128)(2,1)S(1)} %get-tuple-element.20.v_ref, ...), custom_call_target="tpu_custom_call" | custom-call | tf_op jit(solution)/shard_map/forward/pallas_call | solution.py:734
  52.8 11.4 %attend_back.1.g_ref = bf16[8,3,128,128]{3,2,1,0:T(8,128)(2,1)S(1)} custom-call(s32[1,4]{1,0:T(1,128)} %len_ref.3, bf16[16,128,128]{2,1,0:T(8,128)(2,1)S(1)} %get-tuple-element.19.qk_ref, bf16[8,128,128]{2,1,0:T(8,128)(2,1)S(1)} %get-tuple-element.20.v_ref, bf16[8,128,128]{2,1,0:T(8,128)(2,1)S(1)} %get-tuple-element.23.ga_ref), custom_call_target="tpu_custom_call" | custom-call | tf_op jit(solution)/shard_map/attend_back/pallas_call | solution.py:759
  64.2 0.0 copy-done
  64.2 0.0 copy-done.1
  64.2 46.4 %final.1 = (bf16[256,512]{1,0:T(8,128)(2,1)S(1)}, bf16[2,5,4,4,4,16,128]{6,5,4,3,2,1,0:T(8,128)(2,1)S(1)}) custom-call(bf16[8,3,128,128]{3,2,1,0:T(8,128)(2,1)S(1)} %attend_back.1.g_ref, bf16[256,512]{1,0:T(8,128)(2,1)S(1)} %get-tuple-element.21.own_ref, bf16[256,512]{1,0:T(8,128)(2,1)S(1)} %get-tuple-element.24.normed_ref, bf16[512,2048]{1,0:T(8,128)(2,1)S(1)} %copy-done, ...), custom_call_target="tpu_custom_call" | custom-call | tf_op jit(solution)/shard_map/final/pallas_call | solution.py:780
  110.6 2.6 %spread.1 = (f32[512,2048]{1,0:T(8,128)}, f32[512,512]{1,0:T(8,128)}, bf16[256,512]{1,0:T(8,128)(2,1)}, bf16[256,512]{1,0:T(8,128)(2,1)}) custom-call(bf16[2,5,4,4,4,16,128]{6,5,4,3,2,1,0:T(8,128)(2,1)S(1)} %get-tuple-element.27.sum_ref, bf16[256,512]{1,0:T(8,128)(2,1)S(1)} %get-tuple-element.28.layer_ref, bf16[256,512]{1,0:T(8,128)(2,1)S(1)} %get-tuple-element.29.rowgrad_ref), custom_call_target="tpu_custom_call" | custom-call | tf_op jit(solution)/shard_map/spread/pallas_call | solution.py:805
Async XLA Ops:
  0.6 63.5 %copy-start = (bf16[512,2048]{1,0:T(8,128)(2,1)S(1)}, bf16[512,2048]{1,0:T(8,128)(2,1)}, u32[]{:S(2)}) copy-start(bf16[512,2048]{1,0:T(8,128)(2,1)} %w_ref.1) | copy-start | bytes 6291460
  0.6 63.5 %copy-start.1 = (bf16[256,512]{1,0:T(8,128)(2,1)S(1)}, bf16[256,512]{1,0:T(8,128)(2,1)}, u32[]{:S(2)}) copy-start(bf16[256,512]{1,0:T(8,128)(2,1)} %cot_ref.1) | copy-start | bytes 786436

commit v7 on v6

--- a/solution.py
+++ b/solution.py
@@ -617,9 +617,9 @@
         core_start(n + 2)
         return total
 
-    grad_normed = late(0, grad_normed)
     after_core(1)
     after_core(0)
+    grad_normed = late(0, grad_normed)
     grad_normed = late(1, grad_normed)
     grad_normed = late(2, grad_normed)
     after_core(2)

time: 113 us -> 113 us (level)
    pallas_call x1, Pallas kernels: 11.4 us -> 9.82 us  [local(): pl.pallas_call(backward_kernel, name='attend_back', out_shape=shape(NCTX,...]
    pallas_call x1, Pallas kernels: 46.4 us -> 47.6 us  [local(): pl.pallas_call(final_kernel, name='final', out_shape=(shape(BLK, WIDTH),...]
where the time goes in v7:
time: 113 us
  Pallas kernels  112 us (99%)
    pallas_call x1, Pallas kernels, local(): pl.pallas_call(final_kernel, name='final', out_shape=(shape(BLK, WIDTH),...  47.6 us
    pallas_call x1, Pallas kernels, local(): pl.pallas_call(arrive_kernel, name='arrive', out_shape=(shape(BLK, WIDTH)...  33 us
    pallas_call x1, Pallas kernels, local(): pl.pallas_call(forward_kernel, name='forward', out_shape=(shape(BLK, WIDT...  19.1 us
    pallas_call x1, Pallas kernels, local(): pl.pallas_call(backward_kernel, name='attend_back', out_shape=shape(NCTX,...  9.82 us
    pallas_call x1, Pallas kernels, local(): pl.pallas_call(functools.partial(spread_kernel, (BLK * 128) ** (-0.5)), n...  2.59 us

profile of v7, /device:TPU:1, one launch (start us, length us, event | category | flops | bytes accessed | tf_op | source)
XLA Modules:
  0.0 113.0 jit_solution(15313577523080900429)
XLA Ops:
  0.6 0.0 copy-start
  0.6 0.0 copy-start.1
  0.7 33.0 %arrive.1 = (bf16[256,512]{1,0:T(8,128)(2,1)S(1)}, bf16[256,512]{1,0:T(8,128)(2,1)S(1)}, bf16[256,512]{1,0:T(8,128)(2,1)S(1)}, bf16[16,128,128]{2,1,0:T(8,128)(2,1)S(1)}, bf16[8,128,128]{2,1,0:T(8,128)(2,1)S(1)}) custom-call(bf16[256,512]{1,0:T(8,128)(2,1)} %rows_hbm.1, s32[1,256]{1,0:T(1,128)} %bitcast.2, s32[1,256]{1,0:T(1,128)} %bitcast.3, ...), custom_call_target="tpu_custom_call" | custom-call | tf_op jit(solution)/shard_map/arrive/pallas_call | solution.py:704
  33.6 19.1 %forward.1 = (bf16[256,512]{1,0:T(8,128)(2,1)S(1)}, f32[256,512]{1,0:T(8,128)S(1)}, f32[512,512]{1,0:T(8,128)S(1)}, bf16[8,128,128]{2,1,0:T(8,128)(2,1)S(1)}) custom-call(s32[1,4]{1,0:T(1,128)} %len_ref.3, bf16[16,128,128]{2,1,0:T(8,128)(2,1)S(1)} %get-tuple-element.19.qk_ref, bf16[8,128,128]{2,1,0:T(8,128)(2,1)S(1)} %get-tuple-element.20.v_ref, ...), custom_call_target="tpu_custom_call" | custom-call | tf_op jit(solution)/shard_map/forward/pallas_call | solution.py:734
  52.8 9.8 %attend_back.1.g_ref = bf16[8,3,128,128]{3,2,1,0:T(8,128)(2,1)S(1)} custom-call(s32[1,4]{1,0:T(1,128)} %len_ref.3, bf16[16,128,128]{2,1,0:T(8,128)(2,1)S(1)} %get-tuple-element.19.qk_ref, bf16[8,128,128]{2,1,0:T(8,128)(2,1)S(1)} %get-tuple-element.20.v_ref, bf16[8,128,128]{2,1,0:T(8,128)(2,1)S(1)} %get-tuple-element.23.ga_ref), custom_call_target="tpu_custom_call" | custom-call | tf_op jit(solution)/shard_map/attend_back/pallas_call | solution.py:759
  62.6 0.0 copy-done
  62.6 0.0 copy-done.1
  62.6 47.6 %final.1 = (bf16[256,512]{1,0:T(8,128)(2,1)S(1)}, bf16[2,5,4,4,4,16,128]{6,5,4,3,2,1,0:T(8,128)(2,1)S(1)}) custom-call(bf16[8,3,128,128]{3,2,1,0:T(8,128)(2,1)S(1)} %attend_back.1.g_ref, bf16[256,512]{1,0:T(8,128)(2,1)S(1)} %get-tuple-element.21.own_ref, bf16[256,512]{1,0:T(8,128)(2,1)S(1)} %get-tuple-element.24.normed_ref, bf16[512,2048]{1,0:T(8,128)(2,1)S(1)} %copy-done, ...), custom_call_target="tpu_custom_call" | custom-call | tf_op jit(solution)/shard_map/final/pallas_call | solution.py:780
  110.3 2.6 %spread.1 = (f32[512,2048]{1,0:T(8,128)}, f32[512,512]{1,0:T(8,128)}, bf16[256,512]{1,0:T(8,128)(2,1)}, bf16[256,512]{1,0:T(8,128)(2,1)}) custom-call(bf16[2,5,4,4,4,16,128]{6,5,4,3,2,1,0:T(8,128)(2,1)S(1)} %get-tuple-element.27.sum_ref, bf16[256,512]{1,0:T(8,128)(2,1)S(1)} %get-tuple-element.28.layer_ref, bf16[256,512]{1,0:T(8,128)(2,1)S(1)} %get-tuple-element.29.rowgrad_ref), custom_call_target="tpu_custom_call" | custom-call | tf_op jit(solution)/shard_map/spread/pallas_call | solution.py:805
Async XLA Ops:
  0.6 62.0 %copy-start = (bf16[512,2048]{1,0:T(8,128)(2,1)S(1)}, bf16[512,2048]{1,0:T(8,128)(2,1)}, u32[]{:S(2)}) copy-start(bf16[512,2048]{1,0:T(8,128)(2,1)} %w_ref.1) | copy-start | bytes 6291460
  0.6 62.0 %copy-start.1 = (bf16[256,512]{1,0:T(8,128)(2,1)S(1)}, bf16[256,512]{1,0:T(8,128)(2,1)}, u32[]{:S(2)}) copy-start(bf16[256,512]{1,0:T(8,128)(2,1)} %cot_ref.1) | copy-start | bytes 786436
